TPU v7x, 768 devices: a whole 4x8x12 slice. The times are simulated.
768 devices in a mesh: fsdp: 16 (over y, x_hi), tp: 48 (over z, x_lo, core).
Axes of the slice: x: 4 (x_hi: 2, x_lo: 2; x = x_hi * 2 + x_lo), y: 8, z: 12, core: 2. Of those that a mesh axis runs over, the one named last changes fastest.
Arguments:
- tokens: bfloat16 [4608, 8192], P('fsdp'), may hold values from -6 to 6
- norm_gain: bfloat16 [8192], replicated, may hold values from 0.099609375 to 1.8984375
- base: bfloat16 [8192, 18432], P(None, 'tp')
- trained: bfloat16 [8192, 18432], P('fsdp', 'tp')
- exponents: int32 [64, 144], replicated, may hold values from -19 to -14
Outputs:
- gated: bfloat16 [4608, 18432], P('fsdp', 'tp')
All inputs are finite; a program needn't handle non-finite values.
Results may differ from a plain program's by a relative error of at most 0.0053.
Values may be sent and summed in bfloat16 or wider, within the bound.
No kernel may reach another device: no remote copies, remote signals or barrier semaphores. Data moves between devices by JAX's collectives and lax.ppermute only.
A program may use at most 64 MiB of HBM per device.

v0:
```python
import jax
import jax.numpy as jnp
from jax import lax
from jax.sharding import PartitionSpec as P

BLK = 128


clip_limit = 448.0
norm_epsilon = 1e-06
exponent_floor = -19


def power_table(exponents):
    scale = jnp.zeros(exponents.shape, jnp.float32)
    for offset in range(6):
        level = exponent_floor + offset
        scale = scale + jnp.where(exponents == level, jnp.float32(2.0**level), jnp.float32(0.0))
    return scale


def body(tokens, norm_gain, base, trained, exponents):
    columns = base.shape[1]
    own_rows = trained.shape[0]
    rows_wide = tokens.astype(jnp.float32)
    mean_square = jnp.mean(rows_wide * rows_wide, axis=1, keepdims=True)
    normed = (
        rows_wide * lax.rsqrt(mean_square + norm_epsilon) * norm_gain.astype(jnp.float32)
    ).astype(jnp.bfloat16)
    table = power_table(exponents)
    column_start = lax.axis_index("tp") * columns
    column_block = (column_start + jnp.arange(columns, dtype=jnp.int32)) // BLK
    picker = (column_block[None, :] == jnp.arange(table.shape[1], dtype=jnp.int32)[:, None]).astype(
        jnp.float32
    )
    scale_cols = jnp.dot(table, picker, precision=lax.Precision.HIGHEST)
    scale_rows = jnp.repeat(scale_cols, BLK, axis=0).astype(jnp.bfloat16)
    row_start = lax.axis_index("fsdp") * own_rows
    own_base = lax.dynamic_slice_in_dim(base, row_start, own_rows, 0).astype(jnp.float32)
    own_scale = lax.dynamic_slice_in_dim(scale_rows, row_start, own_rows, 0).astype(jnp.float32)
    coded = jnp.clip(
        (trained.astype(jnp.float32) - own_base) / own_scale, -clip_limit, clip_limit
    ).astype(jnp.bfloat16)
    base_rows = base.astype(jnp.float32)
    scale_part = scale_rows.astype(jnp.float32)
    weight = (
        base_rows
        + lax.all_gather(coded, "fsdp", axis=0, tiled=True).astype(jnp.float32) * scale_part
    ).astype(jnp.bfloat16)
    product = jnp.dot(normed, weight, preferred_element_type=jnp.float32)
    return jax.nn.silu(product).astype(jnp.bfloat16)


def solution(mesh):
    placed = (P("fsdp", None), P(), P(None, "tp"), P("fsdp", "tp"), P())
    return jax.shard_map(
        body, mesh=mesh, in_specs=placed, out_specs=P("fsdp", "tp"), check_vma=False
    )
```

profile of v0, /device:TPU:1, one launch (start us, length us, event | category | flops | bytes accessed | tf_op | source)
XLA Modules:
  0.0 164.9 jit_solution(15681175827688763241)
XLA Ops:
  6.5 0.0 copy-start.1
  6.5 0.0 copy-start.2
  6.5 0.0 all-gather.2.cloned.1.call-start
  6.6 1.1 convolution_convert_fusion
  7.7 0.5 broadcast_in_dim.42
  8.3 0.0 copy-start
  8.3 2.6 %copy-done = bf16[64,128,384]{2,1,0:T(8,128)(2,1)} copy-done((bf16[64,128,384]{2,1,0:T(8,128)(2,1)}, bf16[64,128,384]{2,1,0:T(8,128)(2,1)S(1)}, u32[]{:S(2)}) %copy-start) | copy-done | bytes 6291480
  10.9 0.0 copy-done.1
  10.9 2.0 %clamp_convert_fusion = bf16[512,384]{1,0:T(8,128)(2,1)} fusion(bf16[512,384]{1,0:T(8,128)(2,1)S(1)} %copy-done.1, bf16[8192,384]{1,0:T(8,128)(2,1)S(1)} %bitcast.1, s32[]{:T(128)S(6)} %select_n.32, bf16[8192,384]{1,0:T(8,128)(2,1)} %param.7), kind=kLoop, calls=%fused_computation.10 | loop fusion | flops 1376256 | bytes 1572868 | tf_op jit(solution)/shard_map/convert_element_type | solution.py:43
  12.9 0.0 all-gather.2.cloned.1.call-update
  12.9 0.0 copy-done.2
  12.9 3.4 %fusion = f32[288]{0:T(512)S(1)} fusion(bf16[288,8192]{1,0:T(8,128)(2,1)} %param.5), kind=kLoop, calls=%fused_computation.3 | loop fusion | flops 7077600 | bytes 4719744 | tf_op jit(solution)/shard_map/reduce_sum | solution.py:26
  16.3 129.6 %all-gather.2.cloned.1.call-done = bf16[8192,384]{1,0:T(8,128)(2,1)} async-done(((bf16[512,384]{1,0:T(8,128)(2,1)}), bf16[8192,384]{1,0:T(8,128)(2,1)}) %all-gather.2.cloned.1.call-update) | async-done | bytes 6291472 | tf_op jit(solution)/shard_map/all_gather | solution.py:48
  145.9 12.2 %multiply_convert_fusion = bf16[288,384]{1,0:T(8,128)(2,1)} fusion(bf16[8192,384]{1,0:T(8,128)(2,1)} %bitcast.2, bf16[8192,384]{1,0:T(8,128)(2,1)} %all-gather.2.cloned.1.call-done, bf16[8192,384]{1,0:T(8,128)(2,1)} %param.7, bf16[288,8192]{1,0:T(8,128)(2,1)} %param.5, f32[8192]{0:T(1024)S(1)} %convert_element_type.45, f32[288]{0:T(512)S(1)} %add_rsqrt_fusion), kind=kOutput, calls=%fused_computation.11 | convolution fusion | flops 1840803840 | bytes 23848064 | tf_op jit(solution)/shard_map/dot_general | solution.py:50
  (3 shorter events, 0.0 us)
Async XLA Ops:
  6.5 4.4 %copy-start.1 = (bf16[512,384]{1,0:T(8,128)(2,1)S(1)}, bf16[512,384]{1,0:T(8,128)(2,1)}, u32[]{:S(2)}) copy-start(bf16[512,384]{1,0:T(8,128)(2,1)} %param.8) | copy-start | bytes 1179652
  6.5 6.4 %copy-start.2 = (bf16[8192]{0:T(1024)(128)(2,1)S(1)}, bf16[8192]{0:T(1024)(128)(2,1)}, u32[]{:S(2)}) copy-start(bf16[8192]{0:T(1024)(128)(2,1)} %param.6) | copy-start | bytes 49156
  6.5 139.4 %all-gather.2.cloned.1.call-start = ((), (), s32[]{:S(2)}) async-start(), calls=%async_computation | async-start | bytes 6684672 | tf_op jit(solution)/shard_map/all_gather | solution.py:48
  8.3 2.6 %copy-start = (bf16[64,128,384]{2,1,0:T(8,128)(2,1)}, bf16[64,128,384]{2,1,0:T(8,128)(2,1)S(1)}, u32[]{:S(2)}) copy-start(bf16[64,128,384]{2,1,0:T(8,128)(2,1)S(1)} %broadcast_in_dim.42) | copy-start | bytes 18874372
Sparse Core Ops, SparseCore 0:
  13.0 132.8 all-gather.1
where the time goes:
time: 165 us
  waiting for transfers between devices  130 us (79%)
  between operations  13.4 us (8%)
  matrix products  13.3 us (8%)
  other arithmetic  5.35 us (3%)
  local copies, waits for them, and re-layouts  3.19 us (2%)
    all_gather x1, waiting for transfers between devices, body(): lax.all_gather(coded, 'fsdp', axis=0, tiled=True).astype(jnp.float32)  130 us
    dot_general x1, matrix products, body(): product = jnp.dot(normed, weight, preferred_element_type=jnp.float32)  12.2 us
    reduce_sum x1, other arithmetic, body(): mean_square = jnp.mean(rows_wide * rows_wide, axis=1, keepdims=True)  3.35 us
  transfers between devices with their start and end apart: 1, of which 1 were waited for; matrix products, arithmetic and copies ran while one was open for 2% of the time, Pallas kernels for 0%

commit v1 on v0

v1 whole, which is shorter than its diff:
```python
import jax
import jax.numpy as jnp
from jax import lax
from jax.experimental import pallas as pl
from jax.experimental.pallas import tpu as pltpu
from jax.sharding import PartitionSpec as P

BLK = 128

clip_limit = 448.0
norm_epsilon = 1e-06
exponent_floor = -19
lift = 2.0**21


def power(exponent):
    scale = jnp.float32(2.0**exponent_floor)
    for level in range(exponent_floor + 1, exponent_floor + 6):
        scale = jnp.where(exponent == level, jnp.float32(2.0**level), scale)
    return scale


def prepare_kernel(tokens, gain, base, trained, exponents, update, part, x, y, g, b, t, e, sems):
    own_rows, columns = trained.shape
    half_rows, half = part.shape
    pairs = half // own_rows
    f = lax.axis_index("fsdp")
    tp = lax.axis_index("tp")
    side = lax.rem(f, 2)
    core = lax.rem(tp, 2)
    row_blocks, col_blocks = own_rows // BLK, columns // BLK
    first_row = pl.multiple_of(core * half_rows, 16)
    exp_row = pl.multiple_of((f * row_blocks) // 8 * 8, 8)
    exp_copy = pltpu.make_async_copy(exponents.at[pl.ds(exp_row, 8)], e, sems.at[0])
    exp_copy.start()
    base_copy = pltpu.make_async_copy(base.at[pl.ds(pl.multiple_of(f * own_rows, own_rows), own_rows)], b, sems.at[1])
    base_copy.start()
    trained_copy = pltpu.make_async_copy(trained, t, sems.at[2])
    trained_copy.start()
    gain_copy = pltpu.make_async_copy(gain, g, sems.at[3])
    gain_copy.start()

    def column(p):
        return pl.multiple_of((2 * p + 1 - side) * own_rows, own_rows)

    ins = [
        pltpu.make_async_copy(
            tokens.at[pl.ds(first_row, half_rows), pl.ds(column(p), own_rows)],
            x.at[:, pl.ds(p * own_rows, own_rows)],
            sems.at[4 + p],
        )
        for p in range(pairs)
    ]
    for copy in ins:
        copy.start()
    exp_copy.wait()
    base_copy.wait()
    trained_copy.wait()
    for i in range(row_blocks):
        for j in range(col_blocks):
            exponent = e[lax.rem(f * row_blocks, 8) + i, tp * col_blocks + j]
            scale = power(exponent)
            spot = (pl.ds(i * BLK, BLK), pl.ds(j * BLK, BLK))
            diff = t[spot].astype(jnp.float32) - b[spot].astype(jnp.float32)
            coded = jnp.clip(diff * (1.0 / scale), -clip_limit, clip_limit).astype(jnp.bfloat16)
            update[spot] = (coded.astype(jnp.float32) * (scale * lift)).astype(jnp.bfloat16)
    gain_copy.wait()
    outs = [
        pltpu.make_async_copy(
            y.at[:, pl.ds(p * own_rows, own_rows)], part.at[:, pl.ds(p * own_rows, own_rows)], sems.at[4 + pairs + p]
        )
        for p in range(pairs)
    ]
    for p in range(pairs):
        ins[p].wait()
        spot = (slice(None), pl.ds(p * own_rows, own_rows))
        row = g[:, pl.ds(column(p), own_rows)].astype(jnp.float32)
        y[spot] = (x[spot].astype(jnp.float32) * row).astype(jnp.bfloat16)
        outs[p].start()
    for copy in outs:
        copy.wait()


def prepare(tokens, gain, base, trained, exponents):
    rows, depth = tokens.shape
    half_rows, half = rows // 2, depth // 2
    own_rows, columns = trained.shape
    pairs = half // own_rows
    hbm = pl.BlockSpec(memory_space=pltpu.HBM)
    return pl.pallas_call(
        prepare_kernel,
        out_shape=(
            jax.ShapeDtypeStruct((own_rows, columns), jnp.bfloat16),
            jax.ShapeDtypeStruct((half_rows, half), jnp.bfloat16),
        ),
        in_specs=[hbm] * 5,
        out_specs=(pl.BlockSpec(memory_space=pltpu.VMEM), hbm),
        scratch_shapes=[
            pltpu.VMEM((half_rows, half), jnp.bfloat16),
            pltpu.VMEM((half_rows, half), jnp.bfloat16),
            pltpu.VMEM((1, depth), jnp.bfloat16),
            pltpu.VMEM((own_rows, columns), jnp.bfloat16),
            pltpu.VMEM((own_rows, columns), jnp.bfloat16),
            pltpu.SMEM((8, exponents.shape[1]), jnp.int32),
            pltpu.SemaphoreType.DMA((4 + 2 * pairs,)),
        ],
        compiler_params=pltpu.CompilerParams(vmem_limit_bytes=16 * 2**20),
        cost_estimate=pl.CostEstimate(flops=4 * 10**6, bytes_accessed=6 * 10**6, transcendentals=0),
    )(tokens, gain, base, trained, exponents)


def far_kernel(base, delta, got, rest, partial, total):
    step = pl.program_id(0)
    core = lax.rem(lax.axis_index("tp"), 2)
    half_rows = got.shape[0]

    @pl.when(step == 0)
    def _():
        total[...] = jnp.zeros_like(total)

    count, _, own_rows, columns = base.shape
    for i in range(count):
        spot = pl.ds(i * own_rows, own_rows)
        weight = (base[i, 0].astype(jnp.float32) + delta[spot].astype(jnp.float32)).astype(jnp.bfloat16)
        total[0] += jnp.dot(got[:, spot], weight, preferred_element_type=jnp.float32)
        total[1] += jnp.dot(rest[:, spot], weight, preferred_element_type=jnp.float32)

    @pl.when(step == pl.num_programs(0) - 1)
    def _():
        partial[pl.ds(pl.multiple_of(core * half_rows, 16), half_rows)] = total[0].astype(jnp.bfloat16)
        partial[pl.ds(pl.multiple_of((1 - core) * half_rows, 16), half_rows)] = total[1].astype(jnp.bfloat16)


def far_product(base4, delta, got, rest):
    pairs, _, own_rows, columns = base4.shape
    half_rows = got.shape[0]
    count = 2
    return pl.pallas_call(
        far_kernel,
        grid=(pairs // count,),
        out_shape=jax.ShapeDtypeStruct((2 * half_rows, columns), jnp.bfloat16),
        in_specs=[
            pl.BlockSpec((count, 1, own_rows, columns), lambda s: (s, lax.rem(lax.axis_index("fsdp"), 2), 0, 0)),
            pl.BlockSpec((count * own_rows, columns), lambda s: (s, 0)),
            pl.BlockSpec((half_rows, count * own_rows), lambda s: (0, s)),
            pl.BlockSpec((half_rows, count * own_rows), lambda s: (0, s)),
        ],
        out_specs=pl.BlockSpec((2 * half_rows, columns), lambda s: (0, 0)),
        scratch_shapes=[pltpu.VMEM((2, half_rows, columns), jnp.float32)],
        compiler_params=pltpu.CompilerParams(vmem_limit_bytes=16 * 2**20),
        cost_estimate=pl.CostEstimate(flops=10**9, bytes_accessed=9 * 10**6, transcendentals=0),
    )(base4, delta, got, rest)


def near_kernel(tokens, gain, base, delta, product, factor, x, b, d, sems):
    pairs, own_rows, columns = b.shape
    rows, depth = x.shape
    side = lax.rem(lax.axis_index("fsdp"), 2)
    width = 2 * own_rows
    token_copies = [
        pltpu.make_async_copy(
            tokens.at[:, pl.ds(p * width, width)], x.at[:, pl.ds(p * width, width)], sems.at[p]
        )
        for p in range(pairs)
    ]
    base_copies = [pltpu.make_async_copy(base.at[p, side], b.at[p], sems.at[pairs + p]) for p in range(pairs)]
    delta_copies = [
        pltpu.make_async_copy(delta.at[pl.ds(p * own_rows, own_rows)], d.at[p], sems.at[2 * pairs + p])
        for p in range(pairs)
    ]
    for copy in token_copies:
        copy.start()
    for p in range(pairs):
        base_copies[p].start()
        delta_copies[p].start()
    squares = jnp.zeros((rows, BLK), jnp.float32)
    for p in range(pairs):
        token_copies[p].wait()
        for c in range(width // BLK):
            wide = x[:, pl.ds(p * width + c * BLK, BLK)].astype(jnp.float32)
            squares += wide * wide
    mean_square = jnp.sum(squares, axis=1, keepdims=True) * (1.0 / depth)
    scale = lax.rsqrt(mean_square + norm_epsilon)
    factor[...] = jnp.broadcast_to(scale, factor.shape)
    total = jnp.zeros((rows, columns), jnp.float32)
    for p in range(pairs):
        base_copies[p].wait()
        delta_copies[p].wait()
        weight = (b[p].astype(jnp.float32) + d[p].astype(jnp.float32)).astype(jnp.bfloat16)
        spot = pl.ds(pl.multiple_of((2 * p + side) * own_rows, own_rows), own_rows)
        row = gain[:, spot].astype(jnp.float32)
        normed = (x[:, spot].astype(jnp.float32) * scale * row).astype(jnp.bfloat16)
        total += jnp.dot(normed, weight, preferred_element_type=jnp.float32)
    product[...] = total


def near_product(tokens, gain, base4, delta):
    pairs, _, own_rows, columns = base4.shape
    rows, depth = tokens.shape
    hbm = pl.BlockSpec(memory_space=pl.ANY)
    vmem = pl.BlockSpec(memory_space=pltpu.VMEM)
    return pl.pallas_call(
        near_kernel,
        out_shape=(
            jax.ShapeDtypeStruct((rows, columns), jnp.float32),
            jax.ShapeDtypeStruct((rows, BLK), jnp.float32),
        ),
        in_specs=[hbm, vmem, hbm, hbm],
        out_specs=(vmem, vmem),
        scratch_shapes=[
            pltpu.VMEM((rows, depth), jnp.bfloat16),
            pltpu.VMEM((pairs, own_rows, columns), jnp.bfloat16),
            pltpu.VMEM((pairs, own_rows, columns), jnp.bfloat16),
            pltpu.SemaphoreType.DMA((3 * pairs,)),
        ],
        compiler_params=pltpu.CompilerParams(vmem_limit_bytes=24 * 2**20),
        cost_estimate=pl.CostEstimate(flops=10**9, bytes_accessed=12 * 10**6, transcendentals=0),
    )(tokens, gain, base4, delta)


def body(tokens, norm_gain, base, trained, exponents):
    rows, depth = tokens.shape
    columns = base.shape[1]
    own_rows = trained.shape[0]
    sides = depth // own_rows
    pairs = sides // 2
    gain = norm_gain.reshape(1, depth)
    across = [(i, i ^ 1) for i in range(sides)]
    cores = [(i, i ^ 1) for i in range(lax.axis_size("tp"))]
    groups = [list(range(0, sides, 2)), list(range(1, sides, 2))]
    update, part = prepare(tokens, gain, base, trained, exponents)
    got = lax.ppermute(part, "fsdp", across)
    wide = lax.all_gather(update.astype(jnp.float16), "fsdp", axis=0, tiled=True, axis_index_groups=groups)
    wide, got = lax.optimization_barrier((wide, got))
    rest = lax.ppermute(got, "tp", cores)
    delta = (wide.astype(jnp.float32) * (1.0 / lift)).astype(jnp.bfloat16)
    base4 = base.reshape(pairs, 2, own_rows, columns)
    far = lax.ppermute(far_product(base4, delta, got, rest), "fsdp", across)
    near, factor = near_product(tokens, gain, base4, delta)
    product = near + far.astype(jnp.float32) * factor[:, :1]
    return jax.nn.silu(product).astype(jnp.bfloat16)


def solution(mesh):
    placed = (P("fsdp", None), P(), P(None, "tp"), P("fsdp", "tp"), P())
    return jax.shard_map(
        body, mesh=mesh, in_specs=placed, out_specs=P("fsdp", "tp"), check_vma=False
    )
```

time: 165 us -> 76.4 us (0.46)
  waiting for transfers between devices: 130 us -> 1.74 us
  blocking collectives: 0 us -> 33.4 us
  starting transfers between devices: 0.01 us -> 19.5 us
  matrix products: 13.3 us -> 0 us
  between operations: 13.4 us -> 0.11 us
  Pallas kernels: 0 us -> 11.8 us
  local copies, waits for them, and re-layouts: 3.19 us -> 7.84 us
  other arithmetic: 5.35 us -> 1.68 us
    all_gather x1 -> x0, waiting for transfers between devices: 130 us -> none  [body(): lax.all_gather(coded, 'fsdp', axis=0, tiled=True).astype(jnp.float32)]
    all_gather x0 -> x1, blocking collectives: none -> 33.4 us  [body(): lax.all_gather(update.astype(jnp.float16), 'fsdp', axis=0, tiled=True, ax...]
    ppermute x0 -> x3, starting transfers between devices: none -> 19.5 us  [the longest x1 9.15 us: body(): rest = lax.ppermute(got, 'tp', cores)]
    dot_general x2 -> x0, matrix products: 13.3 us -> none  [the longest x1 12.2 us: body(): product = jnp.dot(normed, weight, preferred_element_type=jnp.float32)]
    pallas_call x0 -> x3, Pallas kernels: none -> 11.8 us  [the longest x1 7.57 us: near_product(): pl.pallas_call(near_kernel, out_shape=(jax.ShapeDtypeStruct((rows, column...]
    unnamed x6 -> x14, local copies, waits for them, and re-layouts: 2.64 us -> 6.96 us
    reduce_sum x1 -> x0, other arithmetic: 3.35 us -> none  [body(): mean_square = jnp.mean(rows_wide * rows_wide, axis=1, keepdims=True)]
    ppermute x0 -> x3, waiting for transfers between devices: none -> 1.74 us  [the longest x1 1.74 us: body(): rest = lax.ppermute(got, 'tp', cores)]
  transfers between devices with their start and end apart: 1 -> 3, of which waited for: 1 -> 1; matrix products, arithmetic and copies ran while one was open for 2% -> 1% of each run, Pallas kernels for 0% -> 10%
where the time goes in v1:
time: 76.4 us; the launch traced here: 76.1 us
  blocking collectives  33.4 us (44%)
  starting transfers between devices  19.5 us (26%)
  Pallas kernels  11.8 us (15%)
  local copies, waits for them, and re-layouts  7.84 us (10%)
  waiting for transfers between devices  1.74 us (2%)
  other arithmetic  1.68 us (2%)
    all_gather x1, blocking collectives, body(): lax.all_gather(update.astype(jnp.float16), 'fsdp', axis=0, tiled=True, ax...  33.4 us
    ppermute x1, starting transfers between devices, body(): rest = lax.ppermute(got, 'tp', cores)  9.15 us
    pallas_call x1, Pallas kernels, near_product(): pl.pallas_call(near_kernel, out_shape=(jax.ShapeDtypeStruct((rows, column...  7.57 us
    unnamed x14, local copies, waits for them, and re-layouts  6.96 us
    ppermute x1, starting transfers between devices, body(): got = lax.ppermute(part, 'fsdp', across)  5.48 us
    ppermute x1, starting transfers between devices, body(): far = lax.ppermute(far_product(base4, delta, got, rest), 'fsdp', across)  4.83 us
    pallas_call x1, Pallas kernels, far_product(): pl.pallas_call(far_kernel, grid=(pairs // count,), out_shape=jax.ShapeDty...  2.61 us
    ppermute x1, waiting for transfers between devices, body(): rest = lax.ppermute(got, 'tp', cores)  1.74 us
  transfers between devices with their start and end apart: 3, of which 1 were waited for; matrix products, arithmetic and copies ran while one was open for 1% of the time, Pallas kernels for 10%

profile of v1, /device:TPU:1, one launch (start us, length us, event | category | flops | bytes accessed | tf_op | source)
XLA Modules:
  0.0 76.1 jit_solution(4625405422729347689)
XLA Ops:
  0.0 0.7 reshape.6.gain
  0.7 0.0 copy-start
  0.8 2.8 %copy-done = bf16[8192,384]{1,0:T(8,128)(2,1)S(1)} copy-done((bf16[8192,384]{1,0:T(8,128)(2,1)S(1)}, bf16[8192,384]{1,0:T(8,128)(2,1)}, u32[]{:S(2)}) %copy-start) | copy-done | bytes 6291480
  3.5 0.0 copy-start.2
  3.5 2.3 %copy-done.2 = bf16[288,8192]{1,0:T(8,128)(2,1)S(1)} copy-done((bf16[288,8192]{1,0:T(8,128)(2,1)S(1)}, bf16[288,8192]{1,0:T(8,128)(2,1)}, u32[]{:S(2)}) %copy-start.2) | copy-done | bytes 4718616
  5.9 0.0 copy-start.3
  5.9 1.0 %copy-done.3 = bf16[512,384]{1,0:T(8,128)(2,1)S(1)} copy-done((bf16[512,384]{1,0:T(8,128)(2,1)S(1)}, bf16[512,384]{1,0:T(8,128)(2,1)}, u32[]{:S(2)}) %copy-start.3) | copy-done | bytes 393240
  6.9 0.0 copy-start.4
  6.9 0.8 %copy-done.4 = s32[64,144]{1,0:T(8,128)S(1)} copy-done((s32[64,144]{1,0:T(8,128)S(1)}, s32[64,144]{1,0:T(8,128)}, u32[]{:S(2)}) %copy-start.4) | copy-done | bytes 36888
  7.7 1.6 %shard_map.55 = (bf16[512,384]{1,0:T(8,128)(2,1)S(1)}, bf16[144,4096]{1,0:T(8,128)(2,1)S(1)}) custom-call(bf16[288,8192]{1,0:T(8,128)(2,1)S(1)} %copy-done.2, bf16[1,8192]{1,0:T(2,128)(2,1)S(1)} %reshape.6.gain, bf16[8192,384]{1,0:T(8,128)(2,1)S(1)} %copy-done, bf16[512,384]{1,0:T(8,128)(2,1)S(1)} %copy-done.3, s32[64,144]{1,0:T(8,128)S(1)} %copy-done.4), custom_call_target="tpu_custom_call" | custom-call | flops 4000000 | bytes 6000000 | tf_op jit(solution)/shard_map/pallas_call | solution.py:90
  9.3 5.5 %collective-permute-start = (bf16[144,4096]{1,0:T(8,128)(2,1)S(1)}, bf16[144,4096]{1,0:T(8,128)(2,1)S(1)}, u32[]{:S(2)}, u32[]{:S(2)}) collective-permute-start(bf16[144,4096]{1,0:T(8,128)(2,1)S(1)} %get-tuple-element.12), channel_id=1, source_target_pairs={{0,48},{48,0},{96,144},{144,96},{192,240},{240,192},{288,336},{336... | collective-permute-start | bytes 3538952 | tf_op jit(solution)/shard_map/ppermute | solution.py:232
  14.8 0.1 convert_element_type.15
  14.9 33.4 %all-gather.1 = f16[4096,384]{1,0:T(8,128)(2,1)S(1)} all-gather(f16[512,384]{1,0:T(8,128)(2,1)S(1)} %convert_element_type.15), channel_id=1, replica_groups={{0,96,192,288,384,480,576,672},{48,144,240,336,432,528,624,720},{1,97,1..., dimensions={0}, use_global_device_ids=true | all-gather | bytes 3538944 | tf_op jit(solution)/shard_map/all_gather | solution.py:233
  48.3 0.0 copy-start.1
  48.3 0.0 collective-permute-done.got
  48.3 9.1 %collective-permute-start.1 = (bf16[144,4096]{1,0:T(8,128)(2,1)S(1)}, bf16[144,4096]{1,0:T(8,128)(2,1)S(1)}, u32[]{:S(2)}, u32[]{:S(2)}) collective-permute-start(bf16[144,4096]{1,0:T(8,128)(2,1)S(1)} %collective-permute-done.got), channel_id=1, source_target_pairs={{0,1},{1,0},{2,3},{3,2},{4,5},{5,4},{6,7},{7,6},{8,9},{9,8},{10,11... | collective-permute-start | bytes 3538952 | tf_op jit(solution)/shard_map/ppermute | solution.py:235
  57.5 0.7 multiply_convert_fusion.delta
  58.2 1.7 %collective-permute-done.1.rest = bf16[144,4096]{1,0:T(8,128)(2,1)S(1)} collective-permute-done((bf16[144,4096]{1,0:T(8,128)(2,1)S(1)}, bf16[144,4096]{1,0:T(8,128)(2,1)S(1)}, u32[]{:S(2)}, u32[]{:S(2)}) %collective-permute-start.1) | collective-permute-done | bytes 1179680 | tf_op jit(solution)/shard_map/ppermute | solution.py:235
  59.9 0.0 slice-start
  59.9 0.0 copy-done.1
  59.9 0.0 slice-start.1
  59.9 2.6 %shard_map.57 = bf16[288,384]{1,0:T(8,128)(2,1)S(1)} custom-call(bf16[8,2,512,384]{3,2,1,0:T(8,128)(2,1)S(1)} %bitcast.1, bf16[4096,384]{1,0:T(8,128)(2,1)S(1)} %multiply_convert_fusion.delta, bf16[144,4096]{1,0:T(8,128)(2,1)S(1)} %collective-permute-done.got, bf16[144,4096]{1,0:T(8,128)(2,1)S(1)} %collective-permute-done.1.rest), custom_call_target="tpu_custom_call" | custom-call | flops 1000000000 | bytes 9000000 | tf_op jit(solution)/shard_map/pallas_call | solution.py:138
  62.6 4.8 %collective-permute-start.2 = (bf16[288,384]{1,0:T(8,128)(2,1)S(1)}, bf16[288,384]{1,0:T(8,128)(2,1)S(1)}, u32[]{:S(2)}, u32[]{:S(2)}) collective-permute-start(bf16[288,384]{1,0:T(8,128)(2,1)S(1)} %shard_map.57), channel_id=1, source_target_pairs={{0,48},{48,0},{96,144},{144,96},{192,240},{240,192},{288,336},{336... | collective-permute-start | bytes 663560 | tf_op jit(solution)/shard_map/ppermute | solution.py:238
  67.4 0.0 slice-done
  67.4 0.0 slice-done.1
  67.4 7.6 %shard_map.56 = (f32[288,384]{1,0:T(8,128)S(1)}, f32[288,128]{1,0:T(8,128)S(1)}) custom-call(bf16[288,8192]{1,0:T(8,128)(2,1)S(1)} %bitcast.4, bf16[1,8192]{1,0:T(2,128)(2,1)S(1)} %reshape.6.gain, bf16[8,2,512,384]{3,2,1,0:T(8,128)(2,1)S(1)} %bitcast.2, bf16[4096,384]{1,0:T(8,128)(2,1)S(1)} %multiply_convert_fusion.delta), custom_call_target="tpu_custom_call" | custom-call | flops 1000000000 | bytes 12000000 | tf_op jit(solution)/shard_map/pallas_call | solution.py:202
  75.0 0.1 slice_reduce_fusion
  75.2 0.0 collective-permute-done.2
  75.2 0.9 %multiply_convert_fusion.1 = bf16[288,384]{1,0:T(8,128)(2,1)} fusion(f32[288,384]{1,0:T(8,128)S(1)} %get-tuple-element.14, bf16[288,384]{1,0:T(8,128)(2,1)S(1)} %collective-permute-done.2, f32[288]{0:T(512)S(1)} %slice_reduce_fusion), kind=kLoop, calls=%fused_computation.1 | loop fusion | flops 884736 | bytes 885888 | tf_op jit(solution)/shard_map/convert_element_type | solution.py:241
  (1 shorter events, 0.0 us)
Async XLA Ops:
  0.7 2.8 %copy-start = (bf16[8192,384]{1,0:T(8,128)(2,1)S(1)}, bf16[8192,384]{1,0:T(8,128)(2,1)}, u32[]{:S(2)}) copy-start(bf16[8192,384]{1,0:T(8,128)(2,1)} %base.1) | copy-start | bytes 18874372
  3.5 2.3 %copy-start.2 = (bf16[288,8192]{1,0:T(8,128)(2,1)S(1)}, bf16[288,8192]{1,0:T(8,128)(2,1)}, u32[]{:S(2)}) copy-start(bf16[288,8192]{1,0:T(8,128)(2,1)} %tokens.3) | copy-start | bytes 14155780
  5.9 1.0 %copy-start.3 = (bf16[512,384]{1,0:T(8,128)(2,1)S(1)}, bf16[512,384]{1,0:T(8,128)(2,1)}, u32[]{:S(2)}) copy-start(bf16[512,384]{1,0:T(8,128)(2,1)} %trained.1) | copy-start | bytes 1179652
  6.9 0.8 %copy-start.4 = (s32[64,144]{1,0:T(8,128)S(1)}, s32[64,144]{1,0:T(8,128)}, u32[]{:S(2)}) copy-start(s32[64,144]{1,0:T(8,128)} %exponents.1) | copy-start | bytes 110596
  9.3 39.0 %collective-permute-start = (bf16[144,4096]{1,0:T(8,128)(2,1)S(1)}, bf16[144,4096]{1,0:T(8,128)(2,1)S(1)}, u32[]{:S(2)}, u32[]{:S(2)}) collective-permute-start(bf16[144,4096]{1,0:T(8,128)(2,1)S(1)} %get-tuple-element.12), channel_id=1, source_target_pairs={{0,48},{48,0},{96,144},{144,96},{192,240},{240,192},{288,336},{336... | collective-permute-start | bytes 3538952 | tf_op jit(solution)/shard_map/ppermute | solution.py:232
  48.3 11.6 %copy-start.1 = (bf16[8192,384]{1,0:T(8,128)(2,1)S(1)}, bf16[8192,384]{1,0:T(8,128)(2,1)}, u32[]{:S(2)}) copy-start(bf16[8192,384]{1,0:T(8,128)(2,1)} %base.1) | copy-start | bytes 18874372
  48.3 11.6 %collective-permute-start.1 = (bf16[144,4096]{1,0:T(8,128)(2,1)S(1)}, bf16[144,4096]{1,0:T(8,128)(2,1)S(1)}, u32[]{:S(2)}, u32[]{:S(2)}) collective-permute-start(bf16[144,4096]{1,0:T(8,128)(2,1)S(1)} %collective-permute-done.got), channel_id=1, source_target_pairs={{0,1},{1,0},{2,3},{3,2},{4,5},{5,4},{6,7},{7,6},{8,9},{9,8},{10,11... | collective-permute-start | bytes 3538952 | tf_op jit(solution)/shard_map/ppermute | solution.py:235
  59.9 7.5 %slice-start = ((s8[4718592]{0:T(1024)(128)(4,1)}), s8[4194304]{0:T(1024)(128)(4,1)S(1)}, s32[]{:S(2)}) async-start(s8[4718592]{0:T(1024)(128)(4,1)} %bitcast.3), calls=%async_computation | async-start | bytes 8388608
  59.9 7.5 %slice-start.1 = ((s8[4718592]{0:T(1024)(128)(4,1)}), s8[524288]{0:T(1024)(128)(4,1)S(1)}, s32[]{:S(2)}) async-start(s8[4718592]{0:T(1024)(128)(4,1)} %bitcast.3), calls=%async_computation.1 | async-start | bytes 1048576
  62.6 12.6 %collective-permute-start.2 = (bf16[288,384]{1,0:T(8,128)(2,1)S(1)}, bf16[288,384]{1,0:T(8,128)(2,1)S(1)}, u32[]{:S(2)}, u32[]{:S(2)}) collective-permute-start(bf16[288,384]{1,0:T(8,128)(2,1)S(1)} %shard_map.57), channel_id=1, source_target_pairs={{0,48},{48,0},{96,144},{144,96},{192,240},{240,192},{288,336},{336... | collective-permute-start | bytes 663560 | tf_op jit(solution)/shard_map/ppermute | solution.py:238

commit v2 on v1

v2 whole, which is shorter than its diff:
```python
import jax
import jax.numpy as jnp
from jax import lax
from jax.experimental import pallas as pl
from jax.experimental.pallas import tpu as pltpu
from jax.sharding import PartitionSpec as P

BLK = 128

clip_limit = 448.0
norm_epsilon = 1e-06
exponent_floor = -19
lift = 2.0**21


def power(exponent):
    scale = jnp.float32(2.0**exponent_floor)
    for level in range(exponent_floor + 1, exponent_floor + 6):
        scale = jnp.where(exponent == level, jnp.float32(2.0**level), scale)
    return scale


def prepare_kernel(tokens, base, trained, exponents, update, part, b, t, e, sems):
    own_rows, columns = trained.shape
    half_rows, half = part.shape
    pairs = half // own_rows
    f = lax.axis_index("fsdp")
    tp = lax.axis_index("tp")
    side = lax.rem(f, 2)
    core = lax.rem(tp, 2)
    row_blocks, col_blocks = own_rows // BLK, columns // BLK
    first_row = pl.multiple_of(core * half_rows, 16)
    exp_row = pl.multiple_of((f * row_blocks) // 8 * 8, 8)
    exp_copy = pltpu.make_async_copy(exponents.at[pl.ds(exp_row, 8)], e, sems.at[0])
    exp_copy.start()
    base_copy = pltpu.make_async_copy(base.at[pl.ds(pl.multiple_of(f * own_rows, own_rows), own_rows)], b, sems.at[1])
    base_copy.start()
    trained_copy = pltpu.make_async_copy(trained, t, sems.at[2])
    trained_copy.start()
    token_copies = []
    for p in range(pairs):
        column = pl.multiple_of((2 * p + 1 - side) * own_rows, own_rows)
        copy = pltpu.make_async_copy(
            tokens.at[pl.ds(first_row, half_rows), pl.ds(column, own_rows)],
            part.at[:, pl.ds(p * own_rows, own_rows)],
            sems.at[3 + p],
        )
        copy.start()
        token_copies.append(copy)
    exp_copy.wait()
    base_copy.wait()
    trained_copy.wait()
    for i in range(row_blocks):
        for j in range(col_blocks):
            exponent = e[lax.rem(f * row_blocks, 8) + i, tp * col_blocks + j]
            scale = power(exponent)
            spot = (pl.ds(i * BLK, BLK), pl.ds(j * BLK, BLK))
            diff = t[spot].astype(jnp.float32) - b[spot].astype(jnp.float32)
            coded = jnp.clip(diff * (1.0 / scale), -clip_limit, clip_limit).astype(jnp.bfloat16)
            update[spot] = (coded.astype(jnp.float32) * (scale * lift)).astype(jnp.bfloat16)
    for copy in token_copies:
        copy.wait()


def prepare(tokens, base, trained, exponents):
    rows, depth = tokens.shape
    half_rows, half = rows // 2, depth // 2
    own_rows, columns = trained.shape
    pairs = half // own_rows
    hbm = pl.BlockSpec(memory_space=pl.ANY)
    return pl.pallas_call(
        prepare_kernel,
        out_shape=(
            jax.ShapeDtypeStruct((own_rows, columns), jnp.bfloat16),
            jax.ShapeDtypeStruct((half_rows, half), jnp.bfloat16),
        ),
        in_specs=[hbm] * 4,
        out_specs=(pl.BlockSpec(memory_space=pltpu.VMEM), hbm),
        scratch_shapes=[
            pltpu.VMEM((own_rows, columns), jnp.bfloat16),
            pltpu.VMEM((own_rows, columns), jnp.bfloat16),
            pltpu.SMEM((8, exponents.shape[1]), jnp.int32),
            pltpu.SemaphoreType.DMA((3 + pairs,)),
        ],
        compiler_params=pltpu.CompilerParams(vmem_limit_bytes=60 * 2**20),
        cost_estimate=pl.CostEstimate(flops=4 * 10**6, bytes_accessed=6 * 10**6, transcendentals=0),
    )(tokens, base, trained, exponents)


def far_kernel(base, delta, got, rest, gain, partial, total):
    step = pl.program_id(0)
    core = lax.rem(lax.axis_index("tp"), 2)
    half_rows = got.shape[0]

    @pl.when(step == 0)
    def _():
        total[...] = jnp.zeros_like(total)

    count, _, own_rows, columns = base.shape
    for i in range(count):
        spot = pl.ds(i * own_rows, own_rows)
        row = gain[i, 0].astype(jnp.float32)
        weight = (base[i, 0].astype(jnp.float32) + delta[spot].astype(jnp.float32)).astype(jnp.bfloat16)
        for k, x in enumerate((got, rest)):
            raised = (x[:, spot].astype(jnp.float32) * row).astype(jnp.bfloat16)
            total[k] += jnp.dot(raised, weight, preferred_element_type=jnp.float32)

    @pl.when(step == pl.num_programs(0) - 1)
    def _():
        partial[pl.ds(pl.multiple_of(core * half_rows, 16), half_rows)] = total[0].astype(jnp.bfloat16)
        partial[pl.ds(pl.multiple_of((1 - core) * half_rows, 16), half_rows)] = total[1].astype(jnp.bfloat16)


def far_product(base4, delta, got, rest, gain4):
    pairs, _, own_rows, columns = base4.shape
    half_rows = got.shape[0]
    count = 2
    return pl.pallas_call(
        far_kernel,
        grid=(pairs // count,),
        out_shape=jax.ShapeDtypeStruct((2 * half_rows, columns), jnp.bfloat16),
        in_specs=[
            pl.BlockSpec((count, 1, own_rows, columns), lambda s: (s, lax.rem(lax.axis_index("fsdp"), 2), 0, 0)),
            pl.BlockSpec((count * own_rows, columns), lambda s: (s, 0)),
            pl.BlockSpec((half_rows, count * own_rows), lambda s: (0, s)),
            pl.BlockSpec((half_rows, count * own_rows), lambda s: (0, s)),
            pl.BlockSpec((count, 1, 1, own_rows), lambda s: (s, lax.rem(lax.axis_index("fsdp"), 2), 0, 0)),
        ],
        out_specs=pl.BlockSpec((2 * half_rows, columns), lambda s: (0, 0)),
        scratch_shapes=[pltpu.VMEM((2, half_rows, columns), jnp.float32)],
        compiler_params=pltpu.CompilerParams(vmem_limit_bytes=16 * 2**20),
        cost_estimate=pl.CostEstimate(flops=10**9, bytes_accessed=9 * 10**6, transcendentals=0),
    )(base4, delta, got, rest, gain4)


def factor_kernel(tokens, after, factor, squares):
    step = pl.program_id(0)

    @pl.when(step == 0)
    def _():
        squares[...] = jnp.zeros_like(squares)

    rows, width = tokens.shape
    found = squares[...]
    for c in range(width // BLK):
        wide = tokens[:, pl.ds(c * BLK, BLK)].astype(jnp.float32)
        found += wide * wide
    squares[...] = found

    @pl.when(step == pl.num_programs(0) - 1)
    def _():
        mean_square = jnp.sum(found, axis=1, keepdims=True) * (1.0 / (width * pl.num_programs(0)))
        factor[...] = jnp.broadcast_to(lax.rsqrt(mean_square + norm_epsilon), factor.shape)


def row_factor(tokens, after):
    rows, depth = tokens.shape
    steps = 4
    return pl.pallas_call(
        factor_kernel,
        grid=(steps,),
        out_shape=jax.ShapeDtypeStruct((rows, BLK), jnp.float32),
        in_specs=[pl.BlockSpec((rows, depth // steps), lambda s: (0, s)), pl.BlockSpec(memory_space=pl.ANY)],
        out_specs=pl.BlockSpec((rows, BLK), lambda s: (0, 0)),
        scratch_shapes=[pltpu.VMEM((rows, BLK), jnp.float32)],
        compiler_params=pltpu.CompilerParams(vmem_limit_bytes=16 * 2**20),
        cost_estimate=pl.CostEstimate(flops=5 * 10**6, bytes_accessed=5 * 10**6, transcendentals=0),
    )(tokens, after)


def near_kernel(base, delta, gain, factor, *refs):
    *tokens, product = refs
    step = pl.program_id(0)

    @pl.when(step == 0)
    def _():
        product[...] = jnp.zeros_like(product)

    count, _, own_rows, columns = base.shape
    scale = factor[:, :1]
    for i in range(count):
        spot = pl.ds(i * own_rows, own_rows)
        row = gain[i, 0].astype(jnp.float32)
        weight = (base[i, 0].astype(jnp.float32) + delta[spot].astype(jnp.float32)).astype(jnp.bfloat16)
        normed = (tokens[i][...].astype(jnp.float32) * scale * row).astype(jnp.bfloat16)
        product[...] += jnp.dot(normed, weight, preferred_element_type=jnp.float32)


def near_product(tokens, gain4, base4, delta, factor):
    pairs, _, own_rows, columns = base4.shape
    rows, depth = tokens.shape
    count = 2

    def side():
        return lax.rem(lax.axis_index("fsdp"), 2)

    return pl.pallas_call(
        near_kernel,
        grid=(pairs // count,),
        out_shape=jax.ShapeDtypeStruct((rows, columns), jnp.float32),
        in_specs=[
            pl.BlockSpec((count, 1, own_rows, columns), lambda s: (s, side(), 0, 0)),
            pl.BlockSpec((count * own_rows, columns), lambda s: (s, 0)),
            pl.BlockSpec((count, 1, 1, own_rows), lambda s: (s, side(), 0, 0)),
            pl.BlockSpec((rows, BLK), lambda s: (0, 0)),
        ]
        + [pl.BlockSpec((rows, own_rows), lambda s, i=i: (0, 2 * (count * s + i) + side())) for i in range(count)],
        out_specs=pl.BlockSpec((rows, columns), lambda s: (0, 0)),
        compiler_params=pltpu.CompilerParams(vmem_limit_bytes=16 * 2**20),
        cost_estimate=pl.CostEstimate(flops=10**9, bytes_accessed=9 * 10**6, transcendentals=0),
    )(base4, delta, gain4, factor, *[tokens] * count)


def body(tokens, norm_gain, base, trained, exponents):
    rows, depth = tokens.shape
    columns = base.shape[1]
    own_rows = trained.shape[0]
    sides = depth // own_rows
    pairs = sides // 2
    across = [(i, i ^ 1) for i in range(sides)]
    cores = [(i, i ^ 1) for i in range(lax.axis_size("tp"))]
    groups = [list(range(0, sides, 2)), list(range(1, sides, 2))]
    update, part = prepare(tokens, base, trained, exponents)
    got = lax.ppermute(part, "fsdp", across)
    wide = lax.all_gather(update.astype(jnp.float16), "fsdp", axis=0, tiled=True, axis_index_groups=groups)
    wide, got, late_gain = lax.optimization_barrier((wide, got, norm_gain))
    gain4 = late_gain.reshape(pairs, 2, 1, own_rows)
    rest = lax.ppermute(got, "tp", cores)
    delta = (wide.astype(jnp.float32) * (1.0 / lift)).astype(jnp.bfloat16)
    base4 = base.reshape(pairs, 2, own_rows, columns)
    partial = far_product(base4, delta, got, rest, gain4)
    far = lax.ppermute(partial, "fsdp", across)
    factor = row_factor(tokens, partial)
    near = near_product(tokens, gain4, base4, delta, factor)
    product = near + far.astype(jnp.float32) * factor[:, :1]
    return jax.nn.silu(product).astype(jnp.bfloat16)


def solution(mesh):
    placed = (P("fsdp", None), P(), P(None, "tp"), P("fsdp", "tp"), P())
    return jax.shard_map(
        body, mesh=mesh, in_specs=placed, out_specs=P("fsdp", "tp"), check_vma=False
    )
```

time: 76.4 us -> 106 us (1.39)
  Pallas kernels: 11.8 us -> 45 us
  local copies, waits for them, and re-layouts: 7.84 us -> 1.12 us
  other arithmetic: 1.68 us -> 4.72 us
  starting transfers between devices: 19.5 us -> 21 us
    pallas_call x1, Pallas kernels: 1.6 us -> 37.7 us  [prepare(): pl.pallas_call(prepare_kernel, out_shape=(jax.ShapeDtypeStruct((own_rows,...]
    unnamed x14 -> x8, local copies, waits for them, and re-layouts: 6.96 us -> 0.96 us
    pallas_call x1 -> x2, Pallas kernels: 7.57 us -> 4.51 us  [the longest x1 3.08 us: near_product(): pl.pallas_call(near_kernel, grid=(pairs // count,), out_shape=jax.ShapeDt...]
    convert_element_type x1, other arithmetic: 0.71 us -> 2.75 us  [body(): delta = (wide.astype(jnp.float32) * (1.0 / lift)).astype(jnp.bfloat16)]
    ppermute x1, waiting for transfers between devices: 1.74 us -> 0.01 us  [body(): rest = lax.ppermute(got, 'tp', cores)]
    ppermute x1, starting transfers between devices: 9.15 us -> 10.3 us  [body(): rest = lax.ppermute(got, 'tp', cores)]
    ppermute x1, waiting for transfers between devices: 0.01 us -> 1.06 us  [body(): far = lax.ppermute(partial, 'fsdp', across)]
  transfers between devices with their start and end apart: 3 -> 3, of which waited for: 1 -> 1; matrix products, arithmetic and copies ran while one was open for 1% -> 4% of each run, Pallas kernels for 10% -> 4%
where the time goes in v2:
time: 106 us
  Pallas kernels  45 us (42%)
  blocking collectives  33.2 us (31%)
  starting transfers between devices  21 us (20%)
  other arithmetic  4.72 us (4%)
  local copies, waits for them, and re-layouts  1.12 us (1%)
  waiting for transfers between devices  1.07 us (1%)
    pallas_call x1, Pallas kernels, prepare(): pl.pallas_call(prepare_kernel, out_shape=(jax.ShapeDtypeStruct((own_rows,...  37.7 us
    all_gather x1, blocking collectives, body(): lax.all_gather(update.astype(jnp.float16), 'fsdp', axis=0, tiled=True, ax...  33.2 us
    ppermute x1, starting transfers between devices, body(): rest = lax.ppermute(got, 'tp', cores)  10.3 us
    ppermute x1, starting transfers between devices, body(): got = lax.ppermute(part, 'fsdp', across)  5.48 us
    ppermute x1, starting transfers between devices, body(): far = lax.ppermute(partial, 'fsdp', across)  5.14 us
    pallas_call x1, Pallas kernels, near_product(): pl.pallas_call(near_kernel, grid=(pairs // count,), out_shape=jax.ShapeDt...  3.08 us
    pallas_call x1, Pallas kernels, far_product(): pl.pallas_call(far_kernel, grid=(pairs // count,), out_shape=jax.ShapeDty...  2.78 us
    convert_element_type x1, other arithmetic, body(): delta = (wide.astype(jnp.float32) * (1.0 / lift)).astype(jnp.bfloat16)  2.75 us
  transfers between devices with their start and end apart: 3, of which 1 were waited for; matrix products, arithmetic and copies ran while one was open for 4% of the time, Pallas kernels for 4%

profile of v2, /device:TPU:1, one launch (start us, length us, event | category | flops | bytes accessed | tf_op | source)
XLA Modules:
  0.0 106.1 jit_solution(16981213309241444687)
XLA Ops:
  0.0 37.7 %shard_map.55 = (bf16[512,384]{1,0:T(8,128)(2,1)}, bf16[144,4096]{1,0:T(8,128)(2,1)}) custom-call(bf16[288,8192]{1,0:T(8,128)(2,1)} %refs_1_.1, bf16[8192,384]{1,0:T(8,128)(2,1)} %base.1, bf16[512,384]{1,0:T(8,128)(2,1)} %trained.1, s32[64,144]{1,0:T(8,128)} %exponents.1), custom_call_target="tpu_custom_call" | custom-call | flops 4000000 | bytes 6000000 | tf_op jit(solution)/shard_map/pallas_call | solution.py:71
  37.7 0.0 copy-start.1
  37.7 5.5 %collective-permute-start = (bf16[144,4096]{1,0:T(8,128)(2,1)}, bf16[144,4096]{1,0:T(8,128)(2,1)S(1)}, u32[]{:S(2)}, u32[]{:S(2)}) collective-permute-start(bf16[144,4096]{1,0:T(8,128)(2,1)} %get-tuple-element.11), channel_id=1, source_target_pairs={{0,48},{48,0},{96,144},{144,96},{192,240},{240,192},{288,336},{336... | collective-permute-start | bytes 3538952 | tf_op jit(solution)/shard_map/ppermute | solution.py:224
  43.2 1.1 %convert_element_type.15 = f16[512,384]{1,0:T(8,128)(2,1)S(1)} convert(bf16[512,384]{1,0:T(8,128)(2,1)} %get-tuple-element.10) | non-fusion elementwise | flops 196608 | bytes 786432 | tf_op jit(solution)/shard_map/convert_element_type | solution.py:225
  44.3 33.2 %all-gather.1 = f16[4096,384]{1,0:T(8,128)(2,1)} all-gather(f16[512,384]{1,0:T(8,128)(2,1)S(1)} %convert_element_type.15), channel_id=1, replica_groups={{0,96,192,288,384,480,576,672},{48,144,240,336,432,528,624,720},{1,97,1..., dimensions={0}, use_global_device_ids=true | all-gather | bytes 3538944 | tf_op jit(solution)/shard_map/all_gather | solution.py:225
  77.4 0.0 collective-permute-done.got
  77.4 10.3 %collective-permute-start.1 = (bf16[144,4096]{1,0:T(8,128)(2,1)S(1)}, bf16[144,4096]{1,0:T(8,128)(2,1)S(1)}, u32[]{:S(2)}, u32[]{:S(2)}) collective-permute-start(bf16[144,4096]{1,0:T(8,128)(2,1)S(1)} %collective-permute-done.got), channel_id=1, source_target_pairs={{0,1},{1,0},{2,3},{3,2},{4,5},{5,4},{6,7},{7,6},{8,9},{9,8},{10,11... | collective-permute-start | bytes 3538952 | tf_op jit(solution)/shard_map/ppermute | solution.py:228
  87.8 0.0 copy-done.1
  87.8 0.0 copy-start
  87.8 2.8 %multiply_convert_fusion.delta = bf16[4096,384]{1,0:T(8,128)(2,1)S(1)} fusion(f16[4096,384]{1,0:T(8,128)(2,1)} %all-gather.1), kind=kLoop, calls=%fused_computation | loop fusion | flops 4718592 | bytes 6291456 | tf_op jit(solution)/shard_map/convert_element_type | solution.py:229
  90.6 0.0 collective-permute-done.1.rest
  90.6 0.0 slice-start
  90.6 0.9 copy-done
  91.5 0.0 slice-start.1
  91.5 2.8 %shard_map.56.after = bf16[288,384]{1,0:T(8,128)(2,1)S(1)} custom-call(bf16[8,2,512,384]{3,2,1,0:T(8,128)(2,1)S(1)} %bitcast.3, bf16[4096,384]{1,0:T(8,128)(2,1)S(1)} %multiply_convert_fusion.delta, bf16[144,4096]{1,0:T(8,128)(2,1)S(1)} %collective-permute-done.got, bf16[144,4096]{1,0:T(8,128)(2,1)S(1)} %collective-permute-done.1.rest, ...), custom_call_target="tpu_custom_call" | custom-call | flops 1000000000 | bytes 9000000 | tf_op jit(solution)/shard_map/pallas_call | solution.py:118
  94.3 5.1 %collective-permute-start.2 = (bf16[288,384]{1,0:T(8,128)(2,1)S(1)}, bf16[288,384]{1,0:T(8,128)(2,1)S(1)}, u32[]{:S(2)}, u32[]{:S(2)}) collective-permute-start(bf16[288,384]{1,0:T(8,128)(2,1)S(1)} %shard_map.56.after), channel_id=1, source_target_pairs={{0,48},{48,0},{96,144},{144,96},{192,240},{240,192},{288,336},{336... | collective-permute-start | bytes 663560 | tf_op jit(solution)/shard_map/ppermute | solution.py:232
  99.5 0.0 slice-done
  99.5 0.0 slice-done.1
  99.5 1.4 %shard_map.57.factor = f32[288,128]{1,0:T(8,128)S(1)} custom-call(bf16[288,8192]{1,0:T(8,128)(2,1)S(1)} %bitcast.2, bf16[288,384]{1,0:T(8,128)(2,1)S(1)} %shard_map.56.after), custom_call_target="tpu_custom_call" | custom-call | flops 5000000 | bytes 5000000 | tf_op jit(solution)/shard_map/pallas_call | solution.py:159
  100.9 3.1 %shard_map.58 = f32[288,384]{1,0:T(8,128)S(1)} custom-call(bf16[8,2,512,384]{3,2,1,0:T(8,128)(2,1)S(1)} %bitcast.4, bf16[4096,384]{1,0:T(8,128)(2,1)S(1)} %multiply_convert_fusion.delta, bf16[8,2,1,512]{3,2,1,0:T(2,128)(2,1)S(1)} %reshape.8.gain, f32[288,128]{1,0:T(8,128)S(1)} %shard_map.57.factor, bf16[288,8192]{1,0:T(8,128)(2,1)S(1)} %bitcast.2, ...), custom_call_target="tpu_custom_call" | custom-call | flops 1000000000 | bytes 9000000 | tf_op jit(solution)/shard_map/pallas_call | solution.py:197
  104.0 0.1 slice_reduce_fusion
  104.2 1.1 %collective-permute-done.2 = bf16[288,384]{1,0:T(8,128)(2,1)S(1)} collective-permute-done((bf16[288,384]{1,0:T(8,128)(2,1)S(1)}, bf16[288,384]{1,0:T(8,128)(2,1)S(1)}, u32[]{:S(2)}, u32[]{:S(2)}) %collective-permute-start.2) | collective-permute-done | bytes 221216 | tf_op jit(solution)/shard_map/ppermute | solution.py:232
  105.2 0.9 multiply_convert_fusion.1
  (2 shorter events, 0.0 us)
Async XLA Ops:
  37.7 50.1 %copy-start.1 = (bf16[8192]{0:T(1024)(128)(2,1)S(1)}, bf16[8192]{0:T(1024)(128)(2,1)}, u32[]{:S(2)}) copy-start(bf16[8192]{0:T(1024)(128)(2,1)} %param.6) | copy-start | bytes 49156
  37.7 39.7 %collective-permute-start = (bf16[144,4096]{1,0:T(8,128)(2,1)}, bf16[144,4096]{1,0:T(8,128)(2,1)S(1)}, u32[]{:S(2)}, u32[]{:S(2)}) collective-permute-start(bf16[144,4096]{1,0:T(8,128)(2,1)} %get-tuple-element.11), channel_id=1, source_target_pairs={{0,48},{48,0},{96,144},{144,96},{192,240},{240,192},{288,336},{336... | collective-permute-start | bytes 3538952 | tf_op jit(solution)/shard_map/ppermute | solution.py:224
  77.4 13.1 %collective-permute-start.1 = (bf16[144,4096]{1,0:T(8,128)(2,1)S(1)}, bf16[144,4096]{1,0:T(8,128)(2,1)S(1)}, u32[]{:S(2)}, u32[]{:S(2)}) collective-permute-start(bf16[144,4096]{1,0:T(8,128)(2,1)S(1)} %collective-permute-done.got), channel_id=1, source_target_pairs={{0,1},{1,0},{2,3},{3,2},{4,5},{5,4},{6,7},{7,6},{8,9},{9,8},{10,11... | collective-permute-start | bytes 3538952 | tf_op jit(solution)/shard_map/ppermute | solution.py:228
  87.8 3.7 %copy-start = (bf16[8192,384]{1,0:T(8,128)(2,1)S(1)}, bf16[8192,384]{1,0:T(8,128)(2,1)}, u32[]{:S(2)}) copy-start(bf16[8192,384]{1,0:T(8,128)(2,1)} %base.1) | copy-start | bytes 18874372
  90.6 8.9 %slice-start = ((s8[4718592]{0:T(1024)(128)(4,1)}), s8[4194304]{0:T(1024)(128)(4,1)S(1)}, s32[]{:S(2)}) async-start(s8[4718592]{0:T(1024)(128)(4,1)} %bitcast.1), calls=%async_computation | async-start | bytes 8388608
  91.5 7.9 %slice-start.1 = ((s8[4718592]{0:T(1024)(128)(4,1)}), s8[524288]{0:T(1024)(128)(4,1)S(1)}, s32[]{:S(2)}) async-start(s8[4718592]{0:T(1024)(128)(4,1)} %bitcast.1), calls=%async_computation.1 | async-start | bytes 1048576
  94.3 10.9 %collective-permute-start.2 = (bf16[288,384]{1,0:T(8,128)(2,1)S(1)}, bf16[288,384]{1,0:T(8,128)(2,1)S(1)}, u32[]{:S(2)}, u32[]{:S(2)}) collective-permute-start(bf16[288,384]{1,0:T(8,128)(2,1)S(1)} %shard_map.56.after), channel_id=1, source_target_pairs={{0,48},{48,0},{96,144},{144,96},{192,240},{240,192},{288,336},{336... | collective-permute-start | bytes 663560 | tf_op jit(solution)/shard_map/ppermute | solution.py:232

commit v3 on v2

--- a/solution.py
+++ b/solution.py
@@ -20,7 +20,7 @@
     return scale
 
 
-def prepare_kernel(tokens, base, trained, exponents, update, part, b, t, e, sems):
+def prepare_kernel(tokens, base, trained, exponents, update, part, x, b, t, e, sems):
     own_rows, columns = trained.shape
     half_rows, half = part.shape
     pairs = half // own_rows
@@ -42,11 +42,15 @@
         column = pl.multiple_of((2 * p + 1 - side) * own_rows, own_rows)
         copy = pltpu.make_async_copy(
             tokens.at[pl.ds(first_row, half_rows), pl.ds(column, own_rows)],
-            part.at[:, pl.ds(p * own_rows, own_rows)],
+            x.at[:, pl.ds(p * own_rows, own_rows)],
             sems.at[3 + p],
         )
         copy.start()
         token_copies.append(copy)
+    for copy in token_copies:
+        copy.wait()
+    part_copy = pltpu.make_async_copy(x, part, sems.at[3])
+    part_copy.start()
     exp_copy.wait()
     base_copy.wait()
     trained_copy.wait()
@@ -58,8 +62,7 @@
             diff = t[spot].astype(jnp.float32) - b[spot].astype(jnp.float32)
             coded = jnp.clip(diff * (1.0 / scale), -clip_limit, clip_limit).astype(jnp.bfloat16)
             update[spot] = (coded.astype(jnp.float32) * (scale * lift)).astype(jnp.bfloat16)
-    for copy in token_copies:
-        copy.wait()
+    part_copy.wait()
 
 
 def prepare(tokens, base, trained, exponents):
@@ -77,6 +80,7 @@
         in_specs=[hbm] * 4,
         out_specs=(pl.BlockSpec(memory_space=pltpu.VMEM), hbm),
         scratch_shapes=[
+            pltpu.VMEM((half_rows, half), jnp.bfloat16),
             pltpu.VMEM((own_rows, columns), jnp.bfloat16),
             pltpu.VMEM((own_rows, columns), jnp.bfloat16),
             pltpu.SMEM((8, exponents.shape[1]), jnp.int32),
@@ -99,7 +103,7 @@
     count, _, own_rows, columns = base.shape
     for i in range(count):
         spot = pl.ds(i * own_rows, own_rows)
-        row = gain[i, 0].astype(jnp.float32)
+        row = gain[pl.ds(pl.multiple_of((2 * (count * step + i) + lax.rem(lax.axis_index("fsdp"), 2)) * own_rows, own_rows), own_rows)].astype(jnp.float32).reshape(1, own_rows)
         weight = (base[i, 0].astype(jnp.float32) + delta[spot].astype(jnp.float32)).astype(jnp.bfloat16)
         for k, x in enumerate((got, rest)):
             raised = (x[:, spot].astype(jnp.float32) * row).astype(jnp.bfloat16)
@@ -124,7 +128,7 @@
             pl.BlockSpec((count * own_rows, columns), lambda s: (s, 0)),
             pl.BlockSpec((half_rows, count * own_rows), lambda s: (0, s)),
             pl.BlockSpec((half_rows, count * own_rows), lambda s: (0, s)),
-            pl.BlockSpec((count, 1, 1, own_rows), lambda s: (s, lax.rem(lax.axis_index("fsdp"), 2), 0, 0)),
+            pl.BlockSpec(gain4.shape, lambda s: (0,)),
         ],
         out_specs=pl.BlockSpec((2 * half_rows, columns), lambda s: (0, 0)),
         scratch_shapes=[pltpu.VMEM((2, half_rows, columns), jnp.float32)],
@@ -180,7 +184,7 @@
     scale = factor[:, :1]
     for i in range(count):
         spot = pl.ds(i * own_rows, own_rows)
-        row = gain[i, 0].astype(jnp.float32)
+        row = gain[pl.ds(pl.multiple_of((2 * (count * step + i) + lax.rem(lax.axis_index("fsdp"), 2)) * own_rows, own_rows), own_rows)].astype(jnp.float32).reshape(1, own_rows)
         weight = (base[i, 0].astype(jnp.float32) + delta[spot].astype(jnp.float32)).astype(jnp.bfloat16)
         normed = (tokens[i][...].astype(jnp.float32) * scale * row).astype(jnp.bfloat16)
         product[...] += jnp.dot(normed, weight, preferred_element_type=jnp.float32)
@@ -201,7 +205,7 @@
         in_specs=[
             pl.BlockSpec((count, 1, own_rows, columns), lambda s: (s, side(), 0, 0)),
             pl.BlockSpec((count * own_rows, columns), lambda s: (s, 0)),
-            pl.BlockSpec((count, 1, 1, own_rows), lambda s: (s, side(), 0, 0)),
+            pl.BlockSpec(gain4.shape, lambda s: (0,)),
             pl.BlockSpec((rows, BLK), lambda s: (0, 0)),
         ]
         + [pl.BlockSpec((rows, own_rows), lambda s, i=i: (0, 2 * (count * s + i) + side())) for i in range(count)],
@@ -223,8 +227,9 @@
     update, part = prepare(tokens, base, trained, exponents)
     got = lax.ppermute(part, "fsdp", across)
     wide = lax.all_gather(update.astype(jnp.float16), "fsdp", axis=0, tiled=True, axis_index_groups=groups)
-    wide, got, late_gain = lax.optimization_barrier((wide, got, norm_gain))
-    gain4 = late_gain.reshape(pairs, 2, 1, own_rows)
+    wide, got = lax.optimization_barrier((wide, got))
+    late_gain = norm_gain
+    gain4 = late_gain
     rest = lax.ppermute(got, "tp", cores)
     delta = (wide.astype(jnp.float32) * (1.0 / lift)).astype(jnp.bfloat16)
     base4 = base.reshape(pairs, 2, own_rows, columns)

time: 106 us -> 68.9 us (0.65)
  Pallas kernels: 45 us -> 10.5 us
  other arithmetic: 4.72 us -> 2.75 us
  starting transfers between devices: 21 us -> 19.5 us
  waiting for transfers between devices: 1.07 us -> 2.21 us
    pallas_call x1, Pallas kernels: 37.7 us -> 3.34 us  [prepare(): pl.pallas_call(prepare_kernel, out_shape=(jax.ShapeDtypeStruct((own_rows,...]
    convert_element_type x1, other arithmetic: 2.75 us -> 0.79 us  [body(): delta = (wide.astype(jnp.float32) * (1.0 / lift)).astype(jnp.bfloat16)]
    ppermute x1, waiting for transfers between devices: 0.01 us -> 1.67 us  [body(): rest = lax.ppermute(got, 'tp', cores)]
    ppermute x1, starting transfers between devices: 10.3 us -> 9.15 us  [body(): rest = lax.ppermute(got, 'tp', cores)]
  transfers between devices with their start and end apart: 3 -> 3, of which waited for: 1 -> 2; matrix products, arithmetic and copies ran while one was open for 4% -> 3% of each run, Pallas kernels for 4% -> 7%
where the time goes in v3:
time: 68.9 us; the launch traced here: 68.7 us
  blocking collectives  33.4 us (48%)
  starting transfers between devices  19.5 us (28%)
  Pallas kernels  10.5 us (15%)
  other arithmetic  2.75 us (4%)
  waiting for transfers between devices  2.21 us (3%)
    all_gather x1, blocking collectives, body(): lax.all_gather(update.astype(jnp.float16), 'fsdp', axis=0, tiled=True, ax...  33.4 us
    ppermute x1, starting transfers between devices, body(): rest = lax.ppermute(got, 'tp', cores)  9.15 us
    ppermute x1, starting transfers between devices, body(): got = lax.ppermute(part, 'fsdp', across)  5.48 us
    ppermute x1, starting transfers between devices, body(): far = lax.ppermute(partial, 'fsdp', across)  4.83 us
    pallas_call x1, Pallas kernels, prepare(): pl.pallas_call(prepare_kernel, out_shape=(jax.ShapeDtypeStruct((own_rows,...  3.34 us
    pallas_call x1, Pallas kernels, near_product(): pl.pallas_call(near_kernel, grid=(pairs // count,), out_shape=jax.ShapeDt...  3.04 us
    pallas_call x1, Pallas kernels, far_product(): pl.pallas_call(far_kernel, grid=(pairs // count,), out_shape=jax.ShapeDty...  2.72 us
    ppermute x1, waiting for transfers between devices, body(): rest = lax.ppermute(got, 'tp', cores)  1.67 us
  transfers between devices with their start and end apart: 3, of which 2 were waited for; matrix products, arithmetic and copies ran while one was open for 3% of the time, Pallas kernels for 7%

profile of v3, /device:TPU:1, one launch (start us, length us, event | category | flops | bytes accessed | tf_op | source)
XLA Modules:
  0.0 68.7 jit_solution(8291333814153192159)
XLA Ops:
  0.0 3.3 %shard_map.55 = (bf16[512,384]{1,0:T(8,128)(2,1)}, bf16[144,4096]{1,0:T(8,128)(2,1)}) custom-call(bf16[288,8192]{1,0:T(8,128)(2,1)} %refs_1_.1, bf16[8192,384]{1,0:T(8,128)(2,1)} %base.1, bf16[512,384]{1,0:T(8,128)(2,1)} %trained.1, s32[64,144]{1,0:T(8,128)} %exponents.1), custom_call_target="tpu_custom_call" | custom-call | flops 4000000 | bytes 6000000 | tf_op jit(solution)/shard_map/pallas_call | solution.py:74
  3.3 5.5 %collective-permute-start = (bf16[144,4096]{1,0:T(8,128)(2,1)}, bf16[144,4096]{1,0:T(8,128)(2,1)S(1)}, u32[]{:S(2)}, u32[]{:S(2)}) collective-permute-start(bf16[144,4096]{1,0:T(8,128)(2,1)} %get-tuple-element.10), channel_id=1, source_target_pairs={{0,48},{48,0},{96,144},{144,96},{192,240},{240,192},{288,336},{336... | collective-permute-start | bytes 3538952 | tf_op jit(solution)/shard_map/ppermute | solution.py:228
  8.8 1.1 %convert_element_type.15 = f16[512,384]{1,0:T(8,128)(2,1)S(1)} convert(bf16[512,384]{1,0:T(8,128)(2,1)} %get-tuple-element.9) | non-fusion elementwise | flops 196608 | bytes 786432 | tf_op jit(solution)/shard_map/convert_element_type | solution.py:229
  9.9 0.0 copy-start.1
  9.9 33.4 %all-gather.1 = f16[4096,384]{1,0:T(8,128)(2,1)S(1)} all-gather(f16[512,384]{1,0:T(8,128)(2,1)S(1)} %convert_element_type.15), channel_id=1, replica_groups={{0,96,192,288,384,480,576,672},{48,144,240,336,432,528,624,720},{1,97,1..., dimensions={0}, use_global_device_ids=true | all-gather | bytes 3538944 | tf_op jit(solution)/shard_map/all_gather | solution.py:229
  43.3 0.0 copy-start
  43.4 0.0 collective-permute-done.got
  43.4 9.1 %collective-permute-start.1 = (bf16[144,4096]{1,0:T(8,128)(2,1)S(1)}, bf16[144,4096]{1,0:T(8,128)(2,1)S(1)}, u32[]{:S(2)}, u32[]{:S(2)}) collective-permute-start(bf16[144,4096]{1,0:T(8,128)(2,1)S(1)} %collective-permute-done.got), channel_id=1, source_target_pairs={{0,1},{1,0},{2,3},{3,2},{4,5},{5,4},{6,7},{7,6},{8,9},{9,8},{10,11... | collective-permute-start | bytes 3538952 | tf_op jit(solution)/shard_map/ppermute | solution.py:233
  52.5 0.8 %multiply_convert_fusion.delta = bf16[4096,384]{1,0:T(8,128)(2,1)S(1)} fusion(f16[4096,384]{1,0:T(8,128)(2,1)S(1)} %all-gather.1), kind=kLoop, calls=%fused_computation | loop fusion | flops 4718592 | bytes 6291456 | tf_op jit(solution)/shard_map/convert_element_type | solution.py:234
  53.3 1.7 %collective-permute-done.1.rest = bf16[144,4096]{1,0:T(8,128)(2,1)S(1)} collective-permute-done((bf16[144,4096]{1,0:T(8,128)(2,1)S(1)}, bf16[144,4096]{1,0:T(8,128)(2,1)S(1)}, u32[]{:S(2)}, u32[]{:S(2)}) %collective-permute-start.1) | collective-permute-done | bytes 1179680 | tf_op jit(solution)/shard_map/ppermute | solution.py:233
  55.0 0.0 slice-start
  55.0 0.0 copy-done.1
  55.0 0.0 copy-done
  55.0 0.0 slice-start.1
  55.0 2.7 %shard_map.56.after = bf16[288,384]{1,0:T(8,128)(2,1)S(1)} custom-call(bf16[8,2,512,384]{3,2,1,0:T(8,128)(2,1)S(1)} %bitcast.3, bf16[4096,384]{1,0:T(8,128)(2,1)S(1)} %multiply_convert_fusion.delta, bf16[144,4096]{1,0:T(8,128)(2,1)S(1)} %collective-permute-done.got, bf16[144,4096]{1,0:T(8,128)(2,1)S(1)} %collective-permute-done.1.rest, ...), custom_call_target="tpu_custom_call" | custom-call | flops 1000000000 | bytes 9000000 | tf_op jit(solution)/shard_map/pallas_call | solution.py:122
  57.7 4.8 %collective-permute-start.2 = (bf16[288,384]{1,0:T(8,128)(2,1)S(1)}, bf16[288,384]{1,0:T(8,128)(2,1)S(1)}, u32[]{:S(2)}, u32[]{:S(2)}) collective-permute-start(bf16[288,384]{1,0:T(8,128)(2,1)S(1)} %shard_map.56.after), channel_id=1, source_target_pairs={{0,48},{48,0},{96,144},{144,96},{192,240},{240,192},{288,336},{336... | collective-permute-start | bytes 663560 | tf_op jit(solution)/shard_map/ppermute | solution.py:237
  62.6 0.0 slice-done
  62.6 0.0 slice-done.1
  62.6 1.4 %shard_map.57.factor = f32[288,128]{1,0:T(8,128)S(1)} custom-call(bf16[288,8192]{1,0:T(8,128)(2,1)S(1)} %bitcast.2, bf16[288,384]{1,0:T(8,128)(2,1)S(1)} %shard_map.56.after), custom_call_target="tpu_custom_call" | custom-call | flops 5000000 | bytes 5000000 | tf_op jit(solution)/shard_map/pallas_call | solution.py:163
  64.0 3.0 %shard_map.58 = f32[288,384]{1,0:T(8,128)S(1)} custom-call(bf16[8,2,512,384]{3,2,1,0:T(8,128)(2,1)S(1)} %bitcast.4, bf16[4096,384]{1,0:T(8,128)(2,1)S(1)} %multiply_convert_fusion.delta, bf16[8192]{0:T(1024)(128)(2,1)S(1)} %copy-done.1, f32[288,128]{1,0:T(8,128)S(1)} %shard_map.57.factor, bf16[288,8192]{1,0:T(8,128)(2,1)S(1)} %bitcast.2, ...), custom_call_target="tpu_custom_call" | custom-call | flops 1000000000 | bytes 9000000 | tf_op jit(solution)/shard_map/pallas_call | solution.py:201
  67.1 0.1 slice_reduce_fusion
  67.2 0.5 collective-permute-done.2
  67.8 0.9 %multiply_convert_fusion.1 = bf16[288,384]{1,0:T(8,128)(2,1)} fusion(f32[288,384]{1,0:T(8,128)S(1)} %shard_map.58, bf16[288,384]{1,0:T(8,128)(2,1)S(1)} %collective-permute-done.2, f32[288]{0:T(512)S(1)} %slice_reduce_fusion), kind=kLoop, calls=%fused_computation.1 | loop fusion | flops 884736 | bytes 885888 | tf_op jit(solution)/shard_map/convert_element_type | solution.py:241
  (1 shorter events, 0.0 us)
Async XLA Ops:
  3.3 40.0 %collective-permute-start = (bf16[144,4096]{1,0:T(8,128)(2,1)}, bf16[144,4096]{1,0:T(8,128)(2,1)S(1)}, u32[]{:S(2)}, u32[]{:S(2)}) collective-permute-start(bf16[144,4096]{1,0:T(8,128)(2,1)} %get-tuple-element.10), channel_id=1, source_target_pairs={{0,48},{48,0},{96,144},{144,96},{192,240},{240,192},{288,336},{336... | collective-permute-start | bytes 3538952 | tf_op jit(solution)/shard_map/ppermute | solution.py:228
  9.9 45.1 %copy-start.1 = (bf16[8192]{0:T(1024)(128)(2,1)S(1)}, bf16[8192]{0:T(1024)(128)(2,1)}, u32[]{:S(2)}) copy-start(bf16[8192]{0:T(1024)(128)(2,1)} %gain.3) | copy-start | bytes 49156
  43.3 11.6 %copy-start = (bf16[8192,384]{1,0:T(8,128)(2,1)S(1)}, bf16[8192,384]{1,0:T(8,128)(2,1)}, u32[]{:S(2)}) copy-start(bf16[8192,384]{1,0:T(8,128)(2,1)} %base.1) | copy-start | bytes 18874372
  43.4 11.6 %collective-permute-start.1 = (bf16[144,4096]{1,0:T(8,128)(2,1)S(1)}, bf16[144,4096]{1,0:T(8,128)(2,1)S(1)}, u32[]{:S(2)}, u32[]{:S(2)}) collective-permute-start(bf16[144,4096]{1,0:T(8,128)(2,1)S(1)} %collective-permute-done.got), channel_id=1, source_target_pairs={{0,1},{1,0},{2,3},{3,2},{4,5},{5,4},{6,7},{7,6},{8,9},{9,8},{10,11... | collective-permute-start | bytes 3538952 | tf_op jit(solution)/shard_map/ppermute | solution.py:233
  55.0 7.6 %slice-start = ((s8[4718592]{0:T(1024)(128)(4,1)}), s8[4194304]{0:T(1024)(128)(4,1)S(1)}, s32[]{:S(2)}) async-start(s8[4718592]{0:T(1024)(128)(4,1)} %bitcast.1), calls=%async_computation | async-start | bytes 8388608
  55.0 7.6 %slice-start.1 = ((s8[4718592]{0:T(1024)(128)(4,1)}), s8[524288]{0:T(1024)(128)(4,1)S(1)}, s32[]{:S(2)}) async-start(s8[4718592]{0:T(1024)(128)(4,1)} %bitcast.1), calls=%async_computation.1 | async-start | bytes 1048576
  57.7 10.0 %collective-permute-start.2 = (bf16[288,384]{1,0:T(8,128)(2,1)S(1)}, bf16[288,384]{1,0:T(8,128)(2,1)S(1)}, u32[]{:S(2)}, u32[]{:S(2)}) collective-permute-start(bf16[288,384]{1,0:T(8,128)(2,1)S(1)} %shard_map.56.after), channel_id=1, source_target_pairs={{0,48},{48,0},{96,144},{144,96},{192,240},{240,192},{288,336},{336... | collective-permute-start | bytes 663560 | tf_op jit(solution)/shard_map/ppermute | solution.py:237

commit v4 on v0

v4 whole, which is shorter than its diff:
```python
from functools import partial as partial_of

import jax
import jax.numpy as jnp
from jax import lax
from jax.experimental import pallas as pl
from jax.experimental.pallas import tpu as pltpu
from jax.sharding import PartitionSpec as P

BLK = 128

clip_limit = 448.0
norm_epsilon = 1e-06
exponent_floor = -19
lift = 2.0**21

VMEM = pl.BlockSpec(memory_space=pltpu.VMEM)


def near_memory(x):
    return pltpu.with_memory_space_constraint(x, pltpu.VMEM)


def far_memory(x):
    return pltpu.with_memory_space_constraint(x, pltpu.HBM)


def power(exponent):
    scale = jnp.float32(2.0**exponent_floor)
    for level in range(exponent_floor + 1, exponent_floor + 6):
        scale = jnp.where(exponent == level, jnp.float32(2.0**level), scale)
    return scale


def prepare_kernel(tokens, base, trained, exponents, update, part, b, t, e, sems):
    own_rows, columns = trained.shape
    half_rows, half = part.shape
    pairs = half // own_rows
    f = lax.axis_index("fsdp")
    tp = lax.axis_index("tp")
    side = lax.rem(f, 2)
    core = lax.rem(tp, 2)
    row_blocks, col_blocks = own_rows // BLK, columns // BLK
    first_row = pl.multiple_of(core * half_rows, 16)
    exp_row = pl.multiple_of((f * row_blocks) // 8 * 8, 8)
    exp_copy = pltpu.make_async_copy(exponents.at[pl.ds(exp_row, 8)], e, sems.at[0])
    exp_copy.start()
    base_copy = pltpu.make_async_copy(base.at[pl.ds(pl.multiple_of(f * own_rows, own_rows), own_rows)], b, sems.at[1])
    base_copy.start()
    trained_copy = pltpu.make_async_copy(trained, t, sems.at[2])
    trained_copy.start()
    token_copies = []
    for p in range(pairs):
        column = pl.multiple_of((2 * p + 1 - side) * own_rows, own_rows)
        copy = pltpu.make_async_copy(
            tokens.at[pl.ds(first_row, half_rows), pl.ds(column, own_rows)],
            part.at[:, pl.ds(p * own_rows, own_rows)],
            sems.at[3 + p],
        )
        copy.start()
        token_copies.append(copy)
    exp_copy.wait()
    base_copy.wait()
    trained_copy.wait()
    for i in range(row_blocks):
        for j in range(col_blocks):
            exponent = e[lax.rem(f * row_blocks, 8) + i, tp * col_blocks + j]
            scale = power(exponent)
            spot = (pl.ds(i * BLK, BLK), pl.ds(j * BLK, BLK))
            diff = t[spot].astype(jnp.float32) - b[spot].astype(jnp.float32)
            coded = jnp.clip(diff * (1.0 / scale), -clip_limit, clip_limit).astype(jnp.bfloat16)
            update[spot] = (coded.astype(jnp.float32) * (scale * lift)).astype(jnp.bfloat16)
    for copy in token_copies:
        copy.wait()


def prepare(tokens, base, trained, exponents):
    rows, depth = tokens.shape
    half_rows, half = rows // 2, depth // 2
    own_rows, columns = trained.shape
    pairs = half // own_rows
    hbm = pl.BlockSpec(memory_space=pltpu.HBM)
    return pl.pallas_call(
        prepare_kernel,
        out_shape=(pltpu.VMEM((own_rows, columns), jnp.bfloat16), pltpu.VMEM((half_rows, half), jnp.bfloat16)),
        in_specs=[hbm] * 4,
        out_specs=(VMEM, VMEM),
        scratch_shapes=[
            pltpu.VMEM((own_rows, columns), jnp.bfloat16),
            pltpu.VMEM((own_rows, columns), jnp.bfloat16),
            pltpu.SMEM((8, exponents.shape[1]), jnp.int32),
            pltpu.SemaphoreType.DMA((3 + pairs,)),
        ],
        compiler_params=pltpu.CompilerParams(vmem_limit_bytes=16 * 2**20),
        cost_estimate=pl.CostEstimate(flops=4 * 10**6, bytes_accessed=3 * 10**6, transcendentals=0),
    )(*map(far_memory, (tokens, base, trained, exponents)))


def gain_row(gain, p, own_rows):
    side = lax.rem(lax.axis_index("fsdp"), 2)
    spot = pl.ds(pl.multiple_of((2 * p + side) * own_rows, own_rows), own_rows)
    return gain[spot].astype(jnp.float32).reshape(1, own_rows)


def first_kernel(base, delta, got, gain, weight, first):
    side = lax.rem(lax.axis_index("fsdp"), 2)
    pairs, _, own_rows, columns = base.shape
    total = jnp.zeros(first.shape, jnp.float32)
    for p in range(pairs):
        spot = pl.ds(p * own_rows, own_rows)
        block = (base[p, side].astype(jnp.float32) + delta[spot].astype(jnp.float32)).astype(jnp.bfloat16)
        weight[spot] = block
        raised = (got[:, spot].astype(jnp.float32) * gain_row(gain, p, own_rows)).astype(jnp.bfloat16)
        total += jnp.dot(raised, block, preferred_element_type=jnp.float32)
    first[...] = total.astype(jnp.bfloat16)


def second_kernel(own_rows, weight, rest, gain, first, partial):
    core = lax.rem(lax.axis_index("tp"), 2)
    half_rows, half = rest.shape
    total = jnp.zeros(first.shape, jnp.float32)
    for p in range(half // own_rows):
        spot = pl.ds(p * own_rows, own_rows)
        raised = (rest[:, spot].astype(jnp.float32) * gain_row(gain, p, own_rows)).astype(jnp.bfloat16)
        total += jnp.dot(raised, weight[spot], preferred_element_type=jnp.float32)
    partial[pl.ds(pl.multiple_of(core * half_rows, 16), half_rows)] = first[...]
    partial[pl.ds(pl.multiple_of((1 - core) * half_rows, 16), half_rows)] = total.astype(jnp.bfloat16)


def near_kernel(own_rows, tokens, weight, gain, after, product, factor):
    side = lax.rem(lax.axis_index("fsdp"), 2)
    rows, depth = tokens.shape
    squares = jnp.zeros((rows, BLK), jnp.float32)
    for c in range(depth // BLK):
        wide = tokens[:, pl.ds(c * BLK, BLK)].astype(jnp.float32)
        squares += wide * wide
    scale = lax.rsqrt(jnp.sum(squares, axis=1, keepdims=True) * (1.0 / depth) + norm_epsilon)
    factor[...] = jnp.broadcast_to(scale, factor.shape)
    total = jnp.zeros(product.shape, jnp.float32)
    for p in range(weight.shape[0] // own_rows):
        spot = pl.ds(pl.multiple_of((2 * p + side) * own_rows, own_rows), own_rows)
        normed = (tokens[:, spot].astype(jnp.float32) * scale * gain_row(gain, p, own_rows)).astype(jnp.bfloat16)
        total += jnp.dot(normed, weight[pl.ds(p * own_rows, own_rows)], preferred_element_type=jnp.float32)
    product[...] = total


def call(kernel, out_shape, flops, *operands, extra=()):
    many = isinstance(out_shape, tuple)
    return pl.pallas_call(
        kernel,
        out_shape=out_shape,
        in_specs=[VMEM] * len(operands) + [pl.BlockSpec(memory_space=pl.ANY)] * len(extra),
        out_specs=(VMEM,) * len(out_shape) if many else VMEM,
        compiler_params=pltpu.CompilerParams(vmem_limit_bytes=16 * 2**20),
        cost_estimate=pl.CostEstimate(flops=flops, bytes_accessed=8 * 10**6, transcendentals=0),
    )(*map(near_memory, operands), *extra)


def body(tokens, norm_gain, base, trained, exponents):
    rows, depth = tokens.shape
    columns = base.shape[1]
    own_rows = trained.shape[0]
    sides = depth // own_rows
    pairs = sides // 2
    half_rows, half = rows // 2, depth // 2
    across = [(i, i ^ 1) for i in range(sides)]
    cores = [(i, i ^ 1) for i in range(lax.axis_size("tp"))]
    groups = [list(range(0, sides, 2)), list(range(1, sides, 2))]
    update, part = prepare(tokens, base, trained, exponents)
    got = lax.ppermute(part, "fsdp", across)
    wide = lax.all_gather(update.astype(jnp.float16), "fsdp", axis=0, tiled=True, axis_index_groups=groups)
    wide, got = lax.optimization_barrier((wide, got))
    rest = lax.ppermute(got, "tp", cores)
    delta = (wide.astype(jnp.float32) * (1.0 / lift)).astype(jnp.bfloat16)
    base4 = base.reshape(pairs, 2, own_rows, columns)
    weight, first = call(
        first_kernel,
        (pltpu.VMEM((half, columns), jnp.bfloat16), pltpu.VMEM((half_rows, columns), jnp.bfloat16)),
        5 * 10**8,
        base4,
        delta,
        got,
        norm_gain,
    )
    partial = call(
        partial_of(second_kernel, own_rows), pltpu.VMEM((rows, columns), jnp.bfloat16), 5 * 10**8, weight, rest, norm_gain, first
    )
    far = lax.ppermute(partial, "fsdp", across)

    near, factor = call(
        partial_of(near_kernel, own_rows),
        (pltpu.VMEM((rows, columns), jnp.float32), pltpu.VMEM((rows, BLK), jnp.float32)),
        10**9,
        tokens,
        weight,
        norm_gain,
        extra=(partial,),
    )
    product = near + far.astype(jnp.float32) * factor[:, :1]
    return jax.nn.silu(product).astype(jnp.bfloat16)


def solution(mesh):
    placed = (P("fsdp", None), P(), P(None, "tp"), P("fsdp", "tp"), P())
    return jax.shard_map(
        body, mesh=mesh, in_specs=placed, out_specs=P("fsdp", "tp"), check_vma=False
    )
```

time: 165 us -> 64.2 us (0.39)
  waiting for transfers between devices: 130 us -> 2.95 us
  blocking collectives: 0 us -> 33.4 us
  starting transfers between devices: 0.01 us -> 19.5 us
  matrix products: 13.3 us -> 0 us
  between operations: 13.4 us -> 0.13 us
  Pallas kernels: 0 us -> 6.07 us
  other arithmetic: 5.35 us -> 1.75 us
  local copies, waits for them, and re-layouts: 3.19 us -> 0.17 us
    all_gather x1 -> x0, waiting for transfers between devices: 130 us -> none  [body(): lax.all_gather(coded, 'fsdp', axis=0, tiled=True).astype(jnp.float32)]
    all_gather x0 -> x1, blocking collectives: none -> 33.4 us  [body(): lax.all_gather(update.astype(jnp.float16), 'fsdp', axis=0, tiled=True, ax...]
    ppermute x0 -> x3, starting transfers between devices: none -> 19.5 us  [the longest x1 9.15 us: body(): rest = lax.ppermute(got, 'tp', cores)]
    dot_general x2 -> x0, matrix products: 13.3 us -> none  [the longest x1 12.2 us: body(): product = jnp.dot(normed, weight, preferred_element_type=jnp.float32)]
    pallas_call x0 -> x4, Pallas kernels: none -> 6.07 us  [the longest x3 4.5 us: call(): pl.pallas_call(kernel, out_shape=out_shape, in_specs=[VMEM] * len(operand...]
    reduce_sum x1 -> x0, other arithmetic: 3.35 us -> none  [body(): mean_square = jnp.mean(rows_wide * rows_wide, axis=1, keepdims=True)]
    ppermute x0 -> x3, waiting for transfers between devices: none -> 2.95 us  [the longest x1 2.66 us: body(): far = lax.ppermute(partial, 'fsdp', across)]
    unnamed x6 -> x8, local copies, waits for them, and re-layouts: 2.64 us -> 0.02 us
  transfers between devices with their start and end apart: 1 -> 3, of which waited for: 1 -> 2; matrix products, arithmetic and copies ran while one was open for 2% -> 2% of each run, Pallas kernels for 0% -> 6%
where the time goes in v4:
time: 64.2 us; the launch traced here: 64 us
  blocking collectives  33.4 us (52%)
  starting transfers between devices  19.5 us (30%)
  Pallas kernels  6.07 us (9%)
  waiting for transfers between devices  2.95 us (5%)
  other arithmetic  1.75 us (3%)
    all_gather x1, blocking collectives, body(): lax.all_gather(update.astype(jnp.float16), 'fsdp', axis=0, tiled=True, ax...  33.4 us
    ppermute x1, starting transfers between devices, body(): rest = lax.ppermute(got, 'tp', cores)  9.15 us
    ppermute x1, starting transfers between devices, body(): got = lax.ppermute(part, 'fsdp', across)  5.48 us
    ppermute x1, starting transfers between devices, body(): far = lax.ppermute(partial, 'fsdp', across)  4.83 us
    pallas_call x3, Pallas kernels, call(): pl.pallas_call(kernel, out_shape=out_shape, in_specs=[VMEM] * len(operand...  4.5 us
    ppermute x1, waiting for transfers between devices, body(): far = lax.ppermute(partial, 'fsdp', across)  2.66 us
    pallas_call x1, Pallas kernels, prepare(): pl.pallas_call(prepare_kernel, out_shape=(pltpu.VMEM((own_rows, columns),...  1.56 us
  transfers between devices with their start and end apart: 3, of which 2 were waited for; matrix products, arithmetic and copies ran while one was open for 2% of the time, Pallas kernels for 6%

profile of v4, /device:TPU:1, one launch (start us, length us, event | category | flops | bytes accessed | tf_op | source)
XLA Modules:
  0.0 64.0 jit_solution(290296764713050214)
XLA Ops:
  0.0 1.6 %shard_map.55 = (bf16[512,384]{1,0:T(8,128)(2,1)S(1)}, bf16[144,4096]{1,0:T(8,128)(2,1)S(1)}) custom-call(bf16[288,8192]{1,0:T(8,128)(2,1)} %tokens.3, bf16[8192,384]{1,0:T(8,128)(2,1)} %base.1, bf16[512,384]{1,0:T(8,128)(2,1)} %trained.1, s32[64,144]{1,0:T(8,128)} %exponents.1), custom_call_target="tpu_custom_call" | custom-call | flops 4000000 | bytes 3000000 | tf_op jit(solution)/shard_map/pallas_call | solution.py:83
  1.6 5.5 %collective-permute-start = (bf16[144,4096]{1,0:T(8,128)(2,1)S(1)}, bf16[144,4096]{1,0:T(8,128)(2,1)S(1)}, u32[]{:S(2)}, u32[]{:S(2)}) collective-permute-start(bf16[144,4096]{1,0:T(8,128)(2,1)S(1)} %get-tuple-element.14), channel_id=1, source_target_pairs={{0,48},{48,0},{96,144},{144,96},{192,240},{240,192},{288,336},{336... | collective-permute-start | bytes 3538952 | tf_op jit(solution)/shard_map/ppermute | solution.py:170
  7.1 0.1 convert_element_type.15
  7.1 0.0 copy-start.1
  7.2 33.4 %all-gather.1 = f16[4096,384]{1,0:T(8,128)(2,1)S(1)} all-gather(f16[512,384]{1,0:T(8,128)(2,1)S(1)} %convert_element_type.15), channel_id=1, replica_groups={{0,96,192,288,384,480,576,672},{48,144,240,336,432,528,624,720},{1,97,1..., dimensions={0}, use_global_device_ids=true | all-gather | bytes 3538944 | tf_op jit(solution)/shard_map/all_gather | solution.py:171
  40.6 0.0 copy-start
  40.6 0.0 collective-permute-done.got
  40.6 9.1 %collective-permute-start.1 = (bf16[144,4096]{1,0:T(8,128)(2,1)S(1)}, bf16[144,4096]{1,0:T(8,128)(2,1)S(1)}, u32[]{:S(2)}, u32[]{:S(2)}) collective-permute-start(bf16[144,4096]{1,0:T(8,128)(2,1)S(1)} %collective-permute-done.got), channel_id=1, source_target_pairs={{0,1},{1,0},{2,3},{3,2},{4,5},{5,4},{6,7},{7,6},{8,9},{9,8},{10,11... | collective-permute-start | bytes 3538952 | tf_op jit(solution)/shard_map/ppermute | solution.py:173
  49.7 0.8 %multiply_convert_fusion.delta = bf16[4096,384]{1,0:T(8,128)(2,1)S(1)} fusion(f16[4096,384]{1,0:T(8,128)(2,1)S(1)} %all-gather.1), kind=kLoop, calls=%fused_computation | loop fusion | flops 4718592 | bytes 6291456 | tf_op jit(solution)/shard_map/convert_element_type | solution.py:174
  50.5 0.0 slice-start
  50.5 0.0 copy-done.1
  50.6 0.0 copy-done
  50.6 0.0 slice-start.1
  50.6 1.3 %shard_map.56 = (bf16[4096,384]{1,0:T(8,128)(2,1)S(1)}, bf16[144,384]{1,0:T(8,128)(2,1)S(1)}) custom-call(bf16[8,2,512,384]{3,2,1,0:T(8,128)(2,1)S(1)} %bitcast.1, bf16[4096,384]{1,0:T(8,128)(2,1)S(1)} %multiply_convert_fusion.delta, bf16[144,4096]{1,0:T(8,128)(2,1)S(1)} %collective-permute-done.got, bf16[8192]{0:T(1024)(128)(2,1)S(1)} %copy-done.1), custom_call_target="tpu_custom_call" | custom-call | flops 500000000 | bytes 8000000 | tf_op jit(solution)/shard_map/pallas_call | solution.py:149
  51.9 0.3 collective-permute-done.1.rest
  52.2 0.8 %shard_map.57.after = bf16[288,384]{1,0:T(8,128)(2,1)S(1)} custom-call(bf16[4096,384]{1,0:T(8,128)(2,1)S(1)} %get-tuple-element.17.weight, bf16[144,4096]{1,0:T(8,128)(2,1)S(1)} %collective-permute-done.1.rest, bf16[8192]{0:T(1024)(128)(2,1)S(1)} %copy-done.1, bf16[144,384]{1,0:T(8,128)(2,1)S(1)} %get-tuple-element.18.first), custom_call_target="tpu_custom_call" | custom-call | flops 500000000 | bytes 8000000 | tf_op jit(solution)/shard_map/pallas_call | solution.py:149
  53.0 4.8 %collective-permute-start.2 = (bf16[288,384]{1,0:T(8,128)(2,1)S(1)}, bf16[288,384]{1,0:T(8,128)(2,1)S(1)}, u32[]{:S(2)}, u32[]{:S(2)}) collective-permute-start(bf16[288,384]{1,0:T(8,128)(2,1)S(1)} %shard_map.57.after), channel_id=1, source_target_pairs={{0,48},{48,0},{96,144},{144,96},{192,240},{240,192},{288,336},{336... | collective-permute-start | bytes 663560 | tf_op jit(solution)/shard_map/ppermute | solution.py:188
  57.9 0.0 slice-done
  57.9 0.0 slice-done.1
  57.9 2.4 %shard_map.58 = (f32[288,384]{1,0:T(8,128)S(1)}, f32[288,128]{1,0:T(8,128)S(1)}) custom-call(bf16[288,8192]{1,0:T(8,128)(2,1)S(1)} %bitcast.3, bf16[4096,384]{1,0:T(8,128)(2,1)S(1)} %get-tuple-element.17.weight, bf16[8192]{0:T(1024)(128)(2,1)S(1)} %copy-done.1, bf16[288,384]{1,0:T(8,128)(2,1)S(1)} %shard_map.57.after), custom_call_target="tpu_custom_call" | custom-call | flops 1000000000 | bytes 8000000 | tf_op jit(solution)/shard_map/pallas_call | solution.py:149
  60.3 0.1 slice_reduce_fusion
  60.4 2.7 %collective-permute-done.2 = bf16[288,384]{1,0:T(8,128)(2,1)S(1)} collective-permute-done((bf16[288,384]{1,0:T(8,128)(2,1)S(1)}, bf16[288,384]{1,0:T(8,128)(2,1)S(1)}, u32[]{:S(2)}, u32[]{:S(2)}) %collective-permute-start.2) | collective-permute-done | bytes 221216 | tf_op jit(solution)/shard_map/ppermute | solution.py:188
  63.1 0.9 %multiply_convert_fusion.1 = bf16[288,384]{1,0:T(8,128)(2,1)} fusion(f32[288,384]{1,0:T(8,128)S(1)} %get-tuple-element.19, bf16[288,384]{1,0:T(8,128)(2,1)S(1)} %collective-permute-done.2, f32[288]{0:T(512)S(1)} %slice_reduce_fusion), kind=kLoop, calls=%fused_computation.1 | loop fusion | flops 884736 | bytes 885888 | tf_op jit(solution)/shard_map/convert_element_type | solution.py:200
  (1 shorter events, 0.0 us)
Async XLA Ops:
  1.6 39.0 %collective-permute-start = (bf16[144,4096]{1,0:T(8,128)(2,1)S(1)}, bf16[144,4096]{1,0:T(8,128)(2,1)S(1)}, u32[]{:S(2)}, u32[]{:S(2)}) collective-permute-start(bf16[144,4096]{1,0:T(8,128)(2,1)S(1)} %get-tuple-element.14), channel_id=1, source_target_pairs={{0,48},{48,0},{96,144},{144,96},{192,240},{240,192},{288,336},{336... | collective-permute-start | bytes 3538952 | tf_op jit(solution)/shard_map/ppermute | solution.py:170
  7.1 43.4 %copy-start.1 = (bf16[8192]{0:T(1024)(128)(2,1)S(1)}, bf16[8192]{0:T(1024)(128)(2,1)}, u32[]{:S(2)}) copy-start(bf16[8192]{0:T(1024)(128)(2,1)} %gain.5) | copy-start | bytes 49156
  40.6 10.0 %copy-start = (bf16[8192,384]{1,0:T(8,128)(2,1)S(1)}, bf16[8192,384]{1,0:T(8,128)(2,1)}, u32[]{:S(2)}) copy-start(bf16[8192,384]{1,0:T(8,128)(2,1)} %base.1) | copy-start | bytes 18874372
  40.6 11.6 %collective-permute-start.1 = (bf16[144,4096]{1,0:T(8,128)(2,1)S(1)}, bf16[144,4096]{1,0:T(8,128)(2,1)S(1)}, u32[]{:S(2)}, u32[]{:S(2)}) collective-permute-start(bf16[144,4096]{1,0:T(8,128)(2,1)S(1)} %collective-permute-done.got), channel_id=1, source_target_pairs={{0,1},{1,0},{2,3},{3,2},{4,5},{5,4},{6,7},{7,6},{8,9},{9,8},{10,11... | collective-permute-start | bytes 3538952 | tf_op jit(solution)/shard_map/ppermute | solution.py:173
  50.5 7.3 %slice-start = ((s8[4718592]{0:T(1024)(128)(4,1)}), s8[4194304]{0:T(1024)(128)(4,1)S(1)}, s32[]{:S(2)}) async-start(s8[4718592]{0:T(1024)(128)(4,1)} %bitcast.2), calls=%async_computation | async-start | bytes 8388608
  50.6 7.3 %slice-start.1 = ((s8[4718592]{0:T(1024)(128)(4,1)}), s8[524288]{0:T(1024)(128)(4,1)S(1)}, s32[]{:S(2)}) async-start(s8[4718592]{0:T(1024)(128)(4,1)} %bitcast.2), calls=%async_computation.1 | async-start | bytes 1048576
  53.0 10.0 %collective-permute-start.2 = (bf16[288,384]{1,0:T(8,128)(2,1)S(1)}, bf16[288,384]{1,0:T(8,128)(2,1)S(1)}, u32[]{:S(2)}, u32[]{:S(2)}) collective-permute-start(bf16[288,384]{1,0:T(8,128)(2,1)S(1)} %shard_map.57.after), channel_id=1, source_target_pairs={{0,48},{48,0},{96,144},{144,96},{192,240},{240,192},{288,336},{336... | collective-permute-start | bytes 663560 | tf_op jit(solution)/shard_map/ppermute | solution.py:188

commit v5 on v4

--- a/solution.py
+++ b/solution.py
@@ -118,11 +118,11 @@
 def second_kernel(own_rows, weight, rest, gain, first, partial):
     core = lax.rem(lax.axis_index("tp"), 2)
     half_rows, half = rest.shape
-    total = jnp.zeros(first.shape, jnp.float32)
-    for p in range(half // own_rows):
-        spot = pl.ds(p * own_rows, own_rows)
-        raised = (rest[:, spot].astype(jnp.float32) * gain_row(gain, p, own_rows)).astype(jnp.bfloat16)
-        total += jnp.dot(raised, weight[spot], preferred_element_type=jnp.float32)
+    raised = [
+        (rest[:, pl.ds(p * own_rows, own_rows)].astype(jnp.float32) * gain_row(gain, p, own_rows)).astype(jnp.bfloat16)
+        for p in range(half // own_rows)
+    ]
+    total = jnp.dot(jnp.concatenate(raised, axis=1), weight[...], preferred_element_type=jnp.float32)
     partial[pl.ds(pl.multiple_of(core * half_rows, 16), half_rows)] = first[...]
     partial[pl.ds(pl.multiple_of((1 - core) * half_rows, 16), half_rows)] = total.astype(jnp.bfloat16)
 
@@ -154,6 +154,33 @@
         compiler_params=pltpu.CompilerParams(vmem_limit_bytes=16 * 2**20),
         cost_estimate=pl.CostEstimate(flops=flops, bytes_accessed=8 * 10**6, transcendentals=0),
     )(*map(near_memory, operands), *extra)
+
+
+def last_kernel(near, factor, far, out, done, sems):
+    rows = done.shape[0]
+    count = sems.shape[0]
+    copies = []
+    for i in range(count):
+        spot = pl.ds(i * (rows // count), rows // count)
+        product = near[spot] + far[spot].astype(jnp.float32) * factor[spot, :1]
+        done[spot] = (product / (1.0 + jnp.exp(-product))).astype(jnp.bfloat16)
+        copy = pltpu.make_async_copy(done.at[spot], out.at[spot], sems.at[i])
+        copy.start()
+        copies.append(copy)
+    for copy in copies:
+        copy.wait()
+
+
+def last_step(near, factor, far):
+    return pl.pallas_call(
+        last_kernel,
+        out_shape=jax.ShapeDtypeStruct(near.shape, jnp.bfloat16),
+        in_specs=[VMEM] * 3,
+        out_specs=pl.BlockSpec(memory_space=pl.ANY),
+        scratch_shapes=[pltpu.VMEM(near.shape, jnp.bfloat16), pltpu.SemaphoreType.DMA((3,))],
+        compiler_params=pltpu.CompilerParams(vmem_limit_bytes=16 * 2**20),
+        cost_estimate=pl.CostEstimate(flops=10**6, bytes_accessed=10**6, transcendentals=10**5),
+    )(*map(near_memory, (near, factor, far)))
 
 
 def body(tokens, norm_gain, base, trained, exponents):
@@ -196,8 +223,7 @@
         norm_gain,
         extra=(partial,),
     )
-    product = near + far.astype(jnp.float32) * factor[:, :1]
-    return jax.nn.silu(product).astype(jnp.bfloat16)
+    return last_step(near, factor, far)
 
 
 def solution(mesh):

time: 64.2 us -> 64.2 us (level)
  other arithmetic: 1.75 us -> 0.85 us
  Pallas kernels: 6.07 us -> 6.95 us
    convert_element_type x1 -> x0, other arithmetic: 0.9 us -> none  [body(): return jax.nn.silu(product).astype(jnp.bfloat16)]
    pallas_call x0 -> x1, Pallas kernels: none -> 0.88 us  [last_step(): pl.pallas_call(last_kernel, out_shape=jax.ShapeDtypeStruct(near.shape, jn...]
  transfers between devices with their start and end apart: 3 -> 3, of which waited for: 2 -> 2; matrix products, arithmetic and copies ran while one was open for 2% -> 1% of each run, Pallas kernels for 6% -> 6%
where the time goes in v5:
time: 64.2 us; the launch traced here: 64 us
  blocking collectives  33.4 us (52%)
  starting transfers between devices  19.5 us (30%)
  Pallas kernels  6.95 us (11%)
  waiting for transfers between devices  3.1 us (5%)
  other arithmetic  0.85 us (1%)
    all_gather x1, blocking collectives, body(): lax.all_gather(update.astype(jnp.float16), 'fsdp', axis=0, tiled=True, ax...  33.4 us
    ppermute x1, starting transfers between devices, body(): rest = lax.ppermute(got, 'tp', cores)  9.15 us
    ppermute x1, starting transfers between devices, body(): got = lax.ppermute(part, 'fsdp', across)  5.48 us
    ppermute x1, starting transfers between devices, body(): far = lax.ppermute(partial, 'fsdp', across)  4.83 us
    pallas_call x3, Pallas kernels, call(): pl.pallas_call(kernel, out_shape=out_shape, in_specs=[VMEM] * len(operand...  4.51 us
    ppermute x1, waiting for transfers between devices, body(): far = lax.ppermute(partial, 'fsdp', across)  2.81 us
    pallas_call x1, Pallas kernels, prepare(): pl.pallas_call(prepare_kernel, out_shape=(pltpu.VMEM((own_rows, columns),...  1.56 us
  transfers between devices with their start and end apart: 3, of which 2 were waited for; matrix products, arithmetic and copies ran while one was open for 1% of the time, Pallas kernels for 6%

profile of v5, /device:TPU:1, one launch (start us, length us, event | category | flops | bytes accessed | tf_op | source)
XLA Modules:
  0.0 64.0 jit_solution(4585750115982769450)
XLA Ops:
  0.0 1.6 %shard_map.55 = (bf16[512,384]{1,0:T(8,128)(2,1)S(1)}, bf16[144,4096]{1,0:T(8,128)(2,1)S(1)}) custom-call(bf16[288,8192]{1,0:T(8,128)(2,1)} %tokens.3, bf16[8192,384]{1,0:T(8,128)(2,1)} %base.1, bf16[512,384]{1,0:T(8,128)(2,1)} %trained.1, s32[64,144]{1,0:T(8,128)} %exponents.1), custom_call_target="tpu_custom_call" | custom-call | flops 4000000 | bytes 3000000 | tf_op jit(solution)/shard_map/pallas_call | solution.py:83
  1.6 5.5 %collective-permute-start = (bf16[144,4096]{1,0:T(8,128)(2,1)S(1)}, bf16[144,4096]{1,0:T(8,128)(2,1)S(1)}, u32[]{:S(2)}, u32[]{:S(2)}) collective-permute-start(bf16[144,4096]{1,0:T(8,128)(2,1)S(1)} %get-tuple-element.14), channel_id=1, source_target_pairs={{0,48},{48,0},{96,144},{144,96},{192,240},{240,192},{288,336},{336... | collective-permute-start | bytes 3538952 | tf_op jit(solution)/shard_map/ppermute | solution.py:197
  7.1 0.1 convert_element_type.9
  7.1 0.0 copy-start.1
  7.2 33.4 %all-gather.1 = f16[4096,384]{1,0:T(8,128)(2,1)S(1)} all-gather(f16[512,384]{1,0:T(8,128)(2,1)S(1)} %convert_element_type.9), channel_id=1, replica_groups={{0,96,192,288,384,480,576,672},{48,144,240,336,432,528,624,720},{1,97,1..., dimensions={0}, use_global_device_ids=true | all-gather | bytes 3538944 | tf_op jit(solution)/shard_map/all_gather | solution.py:198
  40.6 0.0 copy-start
  40.6 0.0 collective-permute-done.got
  40.6 9.1 %collective-permute-start.1 = (bf16[144,4096]{1,0:T(8,128)(2,1)S(1)}, bf16[144,4096]{1,0:T(8,128)(2,1)S(1)}, u32[]{:S(2)}, u32[]{:S(2)}) collective-permute-start(bf16[144,4096]{1,0:T(8,128)(2,1)S(1)} %collective-permute-done.got), channel_id=1, source_target_pairs={{0,1},{1,0},{2,3},{3,2},{4,5},{5,4},{6,7},{7,6},{8,9},{9,8},{10,11... | collective-permute-start | bytes 3538952 | tf_op jit(solution)/shard_map/ppermute | solution.py:200
  49.7 0.8 %multiply_convert_fusion.delta = bf16[4096,384]{1,0:T(8,128)(2,1)S(1)} fusion(f16[4096,384]{1,0:T(8,128)(2,1)S(1)} %all-gather.1), kind=kLoop, calls=%fused_computation | loop fusion | flops 4718592 | bytes 6291456 | tf_op jit(solution)/shard_map/convert_element_type | solution.py:201
  50.5 0.0 slice-start
  50.5 0.0 copy-done.1
  50.6 0.0 copy-done
  50.6 0.0 slice-start.1
  50.6 1.3 %shard_map.56 = (bf16[4096,384]{1,0:T(8,128)(2,1)S(1)}, bf16[144,384]{1,0:T(8,128)(2,1)S(1)}) custom-call(bf16[8,2,512,384]{3,2,1,0:T(8,128)(2,1)S(1)} %bitcast.1, bf16[4096,384]{1,0:T(8,128)(2,1)S(1)} %multiply_convert_fusion.delta, bf16[144,4096]{1,0:T(8,128)(2,1)S(1)} %collective-permute-done.got, bf16[8192]{0:T(1024)(128)(2,1)S(1)} %copy-done.1), custom_call_target="tpu_custom_call" | custom-call | flops 500000000 | bytes 8000000 | tf_op jit(solution)/shard_map/pallas_call | solution.py:149
  51.9 0.3 collective-permute-done.1.rest
  52.2 0.8 %shard_map.57.after = bf16[288,384]{1,0:T(8,128)(2,1)S(1)} custom-call(bf16[4096,384]{1,0:T(8,128)(2,1)S(1)} %get-tuple-element.17.weight, bf16[144,4096]{1,0:T(8,128)(2,1)S(1)} %collective-permute-done.1.rest, bf16[8192]{0:T(1024)(128)(2,1)S(1)} %copy-done.1, bf16[144,384]{1,0:T(8,128)(2,1)S(1)} %get-tuple-element.18.first), custom_call_target="tpu_custom_call" | custom-call | flops 500000000 | bytes 8000000 | tf_op jit(solution)/shard_map/pallas_call | solution.py:149
  53.0 4.8 %collective-permute-start.2 = (bf16[288,384]{1,0:T(8,128)(2,1)S(1)}, bf16[288,384]{1,0:T(8,128)(2,1)S(1)}, u32[]{:S(2)}, u32[]{:S(2)}) collective-permute-start(bf16[288,384]{1,0:T(8,128)(2,1)S(1)} %shard_map.57.after), channel_id=1, source_target_pairs={{0,48},{48,0},{96,144},{144,96},{192,240},{240,192},{288,336},{336... | collective-permute-start | bytes 663560 | tf_op jit(solution)/shard_map/ppermute | solution.py:215
  57.9 0.0 slice-done
  57.9 0.0 slice-done.1
  57.9 2.4 %shard_map.58 = (f32[288,384]{1,0:T(8,128)S(1)}, f32[288,128]{1,0:T(8,128)S(1)}) custom-call(bf16[288,8192]{1,0:T(8,128)(2,1)S(1)} %bitcast.3, bf16[4096,384]{1,0:T(8,128)(2,1)S(1)} %get-tuple-element.17.weight, bf16[8192]{0:T(1024)(128)(2,1)S(1)} %copy-done.1, bf16[288,384]{1,0:T(8,128)(2,1)S(1)} %shard_map.57.after), custom_call_target="tpu_custom_call" | custom-call | flops 1000000000 | bytes 8000000 | tf_op jit(solution)/shard_map/pallas_call | solution.py:149
  60.3 2.8 %collective-permute-done.2.far = bf16[288,384]{1,0:T(8,128)(2,1)S(1)} collective-permute-done((bf16[288,384]{1,0:T(8,128)(2,1)S(1)}, bf16[288,384]{1,0:T(8,128)(2,1)S(1)}, u32[]{:S(2)}, u32[]{:S(2)}) %collective-permute-start.2) | collective-permute-done | bytes 221216 | tf_op jit(solution)/shard_map/ppermute | solution.py:215
  63.1 0.9 %shard_map.59 = bf16[288,384]{1,0:T(8,128)(2,1)} custom-call(f32[288,384]{1,0:T(8,128)S(1)} %get-tuple-element.19.near, f32[288,128]{1,0:T(8,128)S(1)} %get-tuple-element.20.factor, bf16[288,384]{1,0:T(8,128)(2,1)S(1)} %collective-permute-done.2.far), custom_call_target="tpu_custom_call" | custom-call | flops 1000000 | bytes 1000000 | tf_op jit(solution)/shard_map/pallas_call | solution.py:175
  (1 shorter events, 0.0 us)
Async XLA Ops:
  1.6 39.0 %collective-permute-start = (bf16[144,4096]{1,0:T(8,128)(2,1)S(1)}, bf16[144,4096]{1,0:T(8,128)(2,1)S(1)}, u32[]{:S(2)}, u32[]{:S(2)}) collective-permute-start(bf16[144,4096]{1,0:T(8,128)(2,1)S(1)} %get-tuple-element.14), channel_id=1, source_target_pairs={{0,48},{48,0},{96,144},{144,96},{192,240},{240,192},{288,336},{336... | collective-permute-start | bytes 3538952 | tf_op jit(solution)/shard_map/ppermute | solution.py:197
  7.1 43.4 %copy-start.1 = (bf16[8192]{0:T(1024)(128)(2,1)S(1)}, bf16[8192]{0:T(1024)(128)(2,1)}, u32[]{:S(2)}) copy-start(bf16[8192]{0:T(1024)(128)(2,1)} %gain.5) | copy-start | bytes 49156
  40.6 10.0 %copy-start = (bf16[8192,384]{1,0:T(8,128)(2,1)S(1)}, bf16[8192,384]{1,0:T(8,128)(2,1)}, u32[]{:S(2)}) copy-start(bf16[8192,384]{1,0:T(8,128)(2,1)} %base.1) | copy-start | bytes 18874372
  40.6 11.6 %collective-permute-start.1 = (bf16[144,4096]{1,0:T(8,128)(2,1)S(1)}, bf16[144,4096]{1,0:T(8,128)(2,1)S(1)}, u32[]{:S(2)}, u32[]{:S(2)}) collective-permute-start(bf16[144,4096]{1,0:T(8,128)(2,1)S(1)} %collective-permute-done.got), channel_id=1, source_target_pairs={{0,1},{1,0},{2,3},{3,2},{4,5},{5,4},{6,7},{7,6},{8,9},{9,8},{10,11... | collective-permute-start | bytes 3538952 | tf_op jit(solution)/shard_map/ppermute | solution.py:200
  50.5 7.3 %slice-start = ((s8[4718592]{0:T(1024)(128)(4,1)}), s8[4194304]{0:T(1024)(128)(4,1)S(1)}, s32[]{:S(2)}) async-start(s8[4718592]{0:T(1024)(128)(4,1)} %bitcast.2), calls=%async_computation | async-start | bytes 8388608
  50.6 7.3 %slice-start.1 = ((s8[4718592]{0:T(1024)(128)(4,1)}), s8[524288]{0:T(1024)(128)(4,1)S(1)}, s32[]{:S(2)}) async-start(s8[4718592]{0:T(1024)(128)(4,1)} %bitcast.2), calls=%async_computation.1 | async-start | bytes 1048576
  53.0 10.1 %collective-permute-start.2 = (bf16[288,384]{1,0:T(8,128)(2,1)S(1)}, bf16[288,384]{1,0:T(8,128)(2,1)S(1)}, u32[]{:S(2)}, u32[]{:S(2)}) collective-permute-start(bf16[288,384]{1,0:T(8,128)(2,1)S(1)} %shard_map.57.after), channel_id=1, source_target_pairs={{0,48},{48,0},{96,144},{144,96},{192,240},{240,192},{288,336},{336... | collective-permute-start | bytes 663560 | tf_op jit(solution)/shard_map/ppermute | solution.py:215

commit v6 on v5

--- a/solution.py
+++ b/solution.py
@@ -34,14 +34,14 @@
 
 def prepare_kernel(tokens, base, trained, exponents, update, part, b, t, e, sems):
     own_rows, columns = trained.shape
-    half_rows, half = part.shape
+    direct_rows, half = part.shape
+    share = direct_rows // 2
     pairs = half // own_rows
     f = lax.axis_index("fsdp")
     tp = lax.axis_index("tp")
     side = lax.rem(f, 2)
     core = lax.rem(tp, 2)
     row_blocks, col_blocks = own_rows // BLK, columns // BLK
-    first_row = pl.multiple_of(core * half_rows, 16)
     exp_row = pl.multiple_of((f * row_blocks) // 8 * 8, 8)
     exp_copy = pltpu.make_async_copy(exponents.at[pl.ds(exp_row, 8)], e, sems.at[0])
     exp_copy.start()
@@ -52,13 +52,22 @@
     token_copies = []
     for p in range(pairs):
         column = pl.multiple_of((2 * p + 1 - side) * own_rows, own_rows)
-        copy = pltpu.make_async_copy(
-            tokens.at[pl.ds(first_row, half_rows), pl.ds(column, own_rows)],
-            part.at[:, pl.ds(p * own_rows, own_rows)],
-            sems.at[3 + p],
-        )
-        copy.start()
-        token_copies.append(copy)
+        here = pl.ds(p * own_rows, own_rows)
+        sem = sems.at[3 + p]
+        whole = pltpu.make_async_copy(tokens.at[pl.ds(0, direct_rows), pl.ds(column, own_rows)], part.at[:, here], sem)
+
+        @pl.when(core == 0)
+        def _(whole=whole):
+            whole.start()
+
+        @pl.when(core == 1)
+        def _(column=column, here=here, sem=sem):
+            for k, row in enumerate((direct_rows, share)):
+                pltpu.make_async_copy(
+                    tokens.at[pl.ds(row, share), pl.ds(column, own_rows)], part.at[pl.ds(k * share, share), here], sem
+                ).start()
+
+        token_copies.append(whole)
     exp_copy.wait()
     base_copy.wait()
     trained_copy.wait()
@@ -76,13 +85,13 @@
 
 def prepare(tokens, base, trained, exponents):
     rows, depth = tokens.shape
-    half_rows, half = rows // 2, depth // 2
+    direct_rows, half = rows // 3 * 2, depth // 2
     own_rows, columns = trained.shape
     pairs = half // own_rows
     hbm = pl.BlockSpec(memory_space=pltpu.HBM)
     return pl.pallas_call(
         prepare_kernel,
-        out_shape=(pltpu.VMEM((own_rows, columns), jnp.bfloat16), pltpu.VMEM((half_rows, half), jnp.bfloat16)),
+        out_shape=(pltpu.VMEM((own_rows, columns), jnp.bfloat16), pltpu.VMEM((direct_rows, half), jnp.bfloat16)),
         in_specs=[hbm] * 4,
         out_specs=(VMEM, VMEM),
         scratch_shapes=[
@@ -117,14 +126,15 @@
 
 def second_kernel(own_rows, weight, rest, gain, first, partial):
     core = lax.rem(lax.axis_index("tp"), 2)
-    half_rows, half = rest.shape
+    share, half = rest.shape
     raised = [
         (rest[:, pl.ds(p * own_rows, own_rows)].astype(jnp.float32) * gain_row(gain, p, own_rows)).astype(jnp.bfloat16)
         for p in range(half // own_rows)
     ]
     total = jnp.dot(jnp.concatenate(raised, axis=1), weight[...], preferred_element_type=jnp.float32)
-    partial[pl.ds(pl.multiple_of(core * half_rows, 16), half_rows)] = first[...]
-    partial[pl.ds(pl.multiple_of((1 - core) * half_rows, 16), half_rows)] = total.astype(jnp.bfloat16)
+    partial[pl.ds(pl.multiple_of(core * 2 * share, 16), share)] = first[:share]
+    partial[pl.ds(share, share)] = first[share:]
+    partial[pl.ds(pl.multiple_of((1 - core) * 2 * share, 16), share)] = total.astype(jnp.bfloat16)
 
 
 def near_kernel(own_rows, tokens, weight, gain, after, product, factor):
@@ -189,7 +199,7 @@
     own_rows = trained.shape[0]
     sides = depth // own_rows
     pairs = sides // 2
-    half_rows, half = rows // 2, depth // 2
+    share, half = rows // 3, depth // 2
     across = [(i, i ^ 1) for i in range(sides)]
     cores = [(i, i ^ 1) for i in range(lax.axis_size("tp"))]
     groups = [list(range(0, sides, 2)), list(range(1, sides, 2))]
@@ -197,12 +207,12 @@
     got = lax.ppermute(part, "fsdp", across)
     wide = lax.all_gather(update.astype(jnp.float16), "fsdp", axis=0, tiled=True, axis_index_groups=groups)
     wide, got = lax.optimization_barrier((wide, got))
-    rest = lax.ppermute(got, "tp", cores)
+    rest = lax.ppermute(got[:share], "tp", cores)
     delta = (wide.astype(jnp.float32) * (1.0 / lift)).astype(jnp.bfloat16)
     base4 = base.reshape(pairs, 2, own_rows, columns)
     weight, first = call(
         first_kernel,
-        (pltpu.VMEM((half, columns), jnp.bfloat16), pltpu.VMEM((half_rows, columns), jnp.bfloat16)),
+        (pltpu.VMEM((half, columns), jnp.bfloat16), pltpu.VMEM((2 * share, columns), jnp.bfloat16)),
         5 * 10**8,
         base4,
         delta,

time: 64.2 us -> 64.5 us (level)
  transfers between devices with their start and end apart: 3 -> 3, of which waited for: 2 -> 1; matrix products, arithmetic and copies ran while one was open for 1% -> 1% of each run, Pallas kernels for 6% -> 6%
where the time goes in v6:
time: 64.5 us; the launch traced here: 64.3 us
  blocking collectives  33.6 us (52%)
  starting transfers between devices  19.4 us (30%)
  Pallas kernels  7.1 us (11%)
  waiting for transfers between devices  3.2 us (5%)
  other arithmetic  0.79 us (1%)
    all_gather x1, blocking collectives, body(): lax.all_gather(update.astype(jnp.float16), 'fsdp', axis=0, tiled=True, ax...  33.6 us
    ppermute x1, starting transfers between devices, body(): rest = lax.ppermute(got[:share], 'tp', cores)  8.89 us
    ppermute x1, starting transfers between devices, body(): got = lax.ppermute(part, 'fsdp', across)  5.61 us
    ppermute x1, starting transfers between devices, body(): far = lax.ppermute(partial, 'fsdp', across)  4.85 us
    pallas_call x3, Pallas kernels, call(): pl.pallas_call(kernel, out_shape=out_shape, in_specs=[VMEM] * len(operand...  4.39 us
    ppermute x1, waiting for transfers between devices, body(): far = lax.ppermute(partial, 'fsdp', across)  3.19 us
    pallas_call x1, Pallas kernels, prepare(): pl.pallas_call(prepare_kernel, out_shape=(pltpu.VMEM((own_rows, columns),...  1.83 us
  transfers between devices with their start and end apart: 3, of which 1 were waited for; matrix products, arithmetic and copies ran while one was open for 1% of the time, Pallas kernels for 6%

profile of v6, /device:TPU:1, one launch (start us, length us, event | category | flops | bytes accessed | tf_op | source)
XLA Modules:
  0.0 64.3 jit_solution(12060066799472608488)
XLA Ops:
  0.0 0.0 slice-start
  0.0 1.8 %shard_map.55 = (bf16[512,384]{1,0:T(8,128)(2,1)S(1)}, bf16[192,4096]{1,0:T(8,128)(2,1)S(1)}) custom-call(bf16[288,8192]{1,0:T(8,128)(2,1)} %tokens.3, bf16[8192,384]{1,0:T(8,128)(2,1)} %base.1, bf16[512,384]{1,0:T(8,128)(2,1)} %trained.1, s32[64,144]{1,0:T(8,128)} %exponents.1), custom_call_target="tpu_custom_call" | custom-call | flops 4000000 | bytes 3000000 | tf_op jit(solution)/shard_map/pallas_call | solution.py:92
  1.8 5.6 %collective-permute-start = (bf16[192,4096]{1,0:T(8,128)(2,1)S(1)}, bf16[192,4096]{1,0:T(8,128)(2,1)S(1)}, u32[]{:S(2)}, u32[]{:S(2)}) collective-permute-start(bf16[192,4096]{1,0:T(8,128)(2,1)S(1)} %get-tuple-element.14), channel_id=1, source_target_pairs={{0,48},{48,0},{96,144},{144,96},{192,240},{240,192},{288,336},{336... | collective-permute-start | bytes 4718600 | tf_op jit(solution)/shard_map/ppermute | solution.py:207
  7.5 0.0 slice-start.1
  7.5 0.1 convert_element_type.9
  7.6 33.6 %all-gather.1 = f16[4096,384]{1,0:T(8,128)(2,1)S(1)} all-gather(f16[512,384]{1,0:T(8,128)(2,1)S(1)} %convert_element_type.9), channel_id=1, replica_groups={{0,96,192,288,384,480,576,672},{48,144,240,336,432,528,624,720},{1,97,1..., dimensions={0}, use_global_device_ids=true | all-gather | bytes 3538944 | tf_op jit(solution)/shard_map/all_gather | solution.py:208
  41.1 0.0 collective-permute-done.got
  41.1 0.1 slice.3
  41.2 0.0 copy-start
  41.2 8.9 %collective-permute-start.1 = (bf16[96,4096]{1,0:T(8,128)(2,1)S(1)}, bf16[96,4096]{1,0:T(8,128)(2,1)S(1)}, u32[]{:S(2)}, u32[]{:S(2)}) collective-permute-start(bf16[96,4096]{1,0:T(8,128)(2,1)S(1)} %slice.3), channel_id=1, source_target_pairs={{0,1},{1,0},{2,3},{3,2},{4,5},{5,4},{6,7},{7,6},{8,9},{9,8},{10,11... | collective-permute-start | bytes 2359304 | tf_op jit(solution)/shard_map/ppermute | solution.py:210
  50.1 0.7 %multiply_convert_fusion.delta = bf16[4096,384]{1,0:T(8,128)(2,1)S(1)} fusion(f16[4096,384]{1,0:T(8,128)(2,1)S(1)} %all-gather.1), kind=kLoop, calls=%fused_computation | loop fusion | flops 4718592 | bytes 6291456 | tf_op jit(solution)/shard_map/convert_element_type | solution.py:211
  50.8 0.0 slice-start.2
  50.8 0.0 slice-done
  50.8 0.0 slice-done.1
  50.9 0.0 copy-done
  50.9 0.0 slice-start.3
  50.9 1.4 %shard_map.56 = (bf16[4096,384]{1,0:T(8,128)(2,1)S(1)}, bf16[192,384]{1,0:T(8,128)(2,1)S(1)}) custom-call(bf16[8,2,512,384]{3,2,1,0:T(8,128)(2,1)S(1)} %bitcast.3, bf16[4096,384]{1,0:T(8,128)(2,1)S(1)} %multiply_convert_fusion.delta, bf16[192,4096]{1,0:T(8,128)(2,1)S(1)} %collective-permute-done.got, bf16[8192]{0:T(1024)(128)(2,1)S(1)} %copy-done), custom_call_target="tpu_custom_call" | custom-call | flops 500000000 | bytes 8000000 | tf_op jit(solution)/shard_map/pallas_call | solution.py:159
  52.3 0.0 collective-permute-done.1.rest
  52.3 0.6 %shard_map.57.after = bf16[288,384]{1,0:T(8,128)(2,1)S(1)} custom-call(bf16[4096,384]{1,0:T(8,128)(2,1)S(1)} %get-tuple-element.17.weight, bf16[96,4096]{1,0:T(8,128)(2,1)S(1)} %collective-permute-done.1.rest, bf16[8192]{0:T(1024)(128)(2,1)S(1)} %copy-done, bf16[192,384]{1,0:T(8,128)(2,1)S(1)} %get-tuple-element.18.first), custom_call_target="tpu_custom_call" | custom-call | flops 500000000 | bytes 8000000 | tf_op jit(solution)/shard_map/pallas_call | solution.py:159
  53.0 4.8 %collective-permute-start.2 = (bf16[288,384]{1,0:T(8,128)(2,1)S(1)}, bf16[288,384]{1,0:T(8,128)(2,1)S(1)}, u32[]{:S(2)}, u32[]{:S(2)}) collective-permute-start(bf16[288,384]{1,0:T(8,128)(2,1)S(1)} %shard_map.57.after), channel_id=1, source_target_pairs={{0,48},{48,0},{96,144},{144,96},{192,240},{240,192},{288,336},{336... | collective-permute-start | bytes 663560 | tf_op jit(solution)/shard_map/ppermute | solution.py:225
  57.8 0.0 slice-done.2
  57.8 0.0 slice-done.3
  57.9 2.3 %shard_map.58 = (f32[288,384]{1,0:T(8,128)S(1)}, f32[288,128]{1,0:T(8,128)S(1)}) custom-call(bf16[288,8192]{1,0:T(8,128)(2,1)S(1)} %bitcast.5, bf16[4096,384]{1,0:T(8,128)(2,1)S(1)} %get-tuple-element.17.weight, bf16[8192]{0:T(1024)(128)(2,1)S(1)} %copy-done, bf16[288,384]{1,0:T(8,128)(2,1)S(1)} %shard_map.57.after), custom_call_target="tpu_custom_call" | custom-call | flops 1000000000 | bytes 8000000 | tf_op jit(solution)/shard_map/pallas_call | solution.py:159
  60.2 3.2 %collective-permute-done.2.far = bf16[288,384]{1,0:T(8,128)(2,1)S(1)} collective-permute-done((bf16[288,384]{1,0:T(8,128)(2,1)S(1)}, bf16[288,384]{1,0:T(8,128)(2,1)S(1)}, u32[]{:S(2)}, u32[]{:S(2)}) %collective-permute-start.2) | collective-permute-done | bytes 221216 | tf_op jit(solution)/shard_map/ppermute | solution.py:225
  63.4 0.9 %shard_map.59 = bf16[288,384]{1,0:T(8,128)(2,1)} custom-call(f32[288,384]{1,0:T(8,128)S(1)} %get-tuple-element.19.near, f32[288,128]{1,0:T(8,128)S(1)} %get-tuple-element.20.factor, bf16[288,384]{1,0:T(8,128)(2,1)S(1)} %collective-permute-done.2.far), custom_call_target="tpu_custom_call" | custom-call | flops 1000000 | bytes 1000000 | tf_op jit(solution)/shard_map/pallas_call | solution.py:185
  (2 shorter events, 0.0 us)
Async XLA Ops:
  0.0 50.8 %slice-start = ((s8[6291456]{0:T(1024)(128)(4,1)}), s8[4194304]{0:T(1024)(128)(4,1)S(1)}, s32[]{:S(2)}) async-start(s8[6291456]{0:T(1024)(128)(4,1)} %bitcast.1), calls=%async_computation | async-start | bytes 8388608
  1.8 39.3 %collective-permute-start = (bf16[192,4096]{1,0:T(8,128)(2,1)S(1)}, bf16[192,4096]{1,0:T(8,128)(2,1)S(1)}, u32[]{:S(2)}, u32[]{:S(2)}) collective-permute-start(bf16[192,4096]{1,0:T(8,128)(2,1)S(1)} %get-tuple-element.14), channel_id=1, source_target_pairs={{0,48},{48,0},{96,144},{144,96},{192,240},{240,192},{288,336},{336... | collective-permute-start | bytes 4718600 | tf_op jit(solution)/shard_map/ppermute | solution.py:207
  7.5 43.4 %slice-start.1 = ((s8[6291456]{0:T(1024)(128)(4,1)}), s8[2097152]{0:T(1024)(128)(4,1)S(1)}, s32[]{:S(2)}) async-start(s8[6291456]{0:T(1024)(128)(4,1)} %bitcast.1), calls=%async_computation.1 | async-start | bytes 4194304
  41.2 9.7 %copy-start = (bf16[8192]{0:T(1024)(128)(2,1)S(1)}, bf16[8192]{0:T(1024)(128)(2,1)}, u32[]{:S(2)}) copy-start(bf16[8192]{0:T(1024)(128)(2,1)} %gain.5) | copy-start | bytes 49156
  41.2 11.1 %collective-permute-start.1 = (bf16[96,4096]{1,0:T(8,128)(2,1)S(1)}, bf16[96,4096]{1,0:T(8,128)(2,1)S(1)}, u32[]{:S(2)}, u32[]{:S(2)}) collective-permute-start(bf16[96,4096]{1,0:T(8,128)(2,1)S(1)} %slice.3), channel_id=1, source_target_pairs={{0,1},{1,0},{2,3},{3,2},{4,5},{5,4},{6,7},{7,6},{8,9},{9,8},{10,11... | collective-permute-start | bytes 2359304 | tf_op jit(solution)/shard_map/ppermute | solution.py:210
  50.8 7.0 %slice-start.2 = ((s8[4718592]{0:T(1024)(128)(4,1)}), s8[4194304]{0:T(1024)(128)(4,1)S(1)}, s32[]{:S(2)}) async-start(s8[4718592]{0:T(1024)(128)(4,1)} %bitcast.4), calls=%async_computation.2 | async-start | bytes 8388608
  50.9 7.0 %slice-start.3 = ((s8[4718592]{0:T(1024)(128)(4,1)}), s8[524288]{0:T(1024)(128)(4,1)S(1)}, s32[]{:S(2)}) async-start(s8[4718592]{0:T(1024)(128)(4,1)} %bitcast.4), calls=%async_computation.3 | async-start | bytes 1048576
  53.0 10.4 %collective-permute-start.2 = (bf16[288,384]{1,0:T(8,128)(2,1)S(1)}, bf16[288,384]{1,0:T(8,128)(2,1)S(1)}, u32[]{:S(2)}, u32[]{:S(2)}) collective-permute-start(bf16[288,384]{1,0:T(8,128)(2,1)S(1)} %shard_map.57.after), channel_id=1, source_target_pairs={{0,48},{48,0},{96,144},{144,96},{192,240},{240,192},{288,336},{336... | collective-permute-start | bytes 663560 | tf_op jit(solution)/shard_map/ppermute | solution.py:225

commit v7 on v5

--- a/solution.py
+++ b/solution.py
@@ -57,7 +57,7 @@
             part.at[:, pl.ds(p * own_rows, own_rows)],
             sems.at[3 + p],
         )
-        copy.start()
+        copy.start(priority=p % 2)
         token_copies.append(copy)
     exp_copy.wait()
     base_copy.wait()

time: 64.2 us -> 64.2 us (level)
  no operation moved by 1% of the time
where the time goes in v7:
time: 64.2 us; the launch traced here: 64 us
  blocking collectives  33.4 us (52%)
  starting transfers between devices  19.5 us (30%)
  Pallas kernels  7.04 us (11%)
  waiting for transfers between devices  3.08 us (5%)
  other arithmetic  0.85 us (1%)
    all_gather x1, blocking collectives, body(): lax.all_gather(update.astype(jnp.float16), 'fsdp', axis=0, tiled=True, ax...  33.4 us
    ppermute x1, starting transfers between devices, body(): rest = lax.ppermute(got, 'tp', cores)  9.15 us
    ppermute x1, starting transfers between devices, body(): got = lax.ppermute(part, 'fsdp', across)  5.48 us
    ppermute x1, starting transfers between devices, body(): far = lax.ppermute(partial, 'fsdp', across)  4.83 us
    pallas_call x3, Pallas kernels, call(): pl.pallas_call(kernel, out_shape=out_shape, in_specs=[VMEM] * len(operand...  4.52 us
    ppermute x1, waiting for transfers between devices, body(): far = lax.ppermute(partial, 'fsdp', across)  2.78 us
    pallas_call x1, Pallas kernels, prepare(): pl.pallas_call(prepare_kernel, out_shape=(pltpu.VMEM((own_rows, columns),...  1.64 us
  transfers between devices with their start and end apart: 3, of which 2 were waited for; matrix products, arithmetic and copies ran while one was open for 1% of the time, Pallas kernels for 6%

profile of v7, /device:TPU:1, one launch (start us, length us, event | category | flops | bytes accessed | tf_op | source)
XLA Modules:
  0.0 64.0 jit_solution(6389889709327631677)
XLA Ops:
  0.0 1.6 %shard_map.55 = (bf16[512,384]{1,0:T(8,128)(2,1)S(1)}, bf16[144,4096]{1,0:T(8,128)(2,1)S(1)}) custom-call(bf16[288,8192]{1,0:T(8,128)(2,1)} %tokens.3, bf16[8192,384]{1,0:T(8,128)(2,1)} %base.1, bf16[512,384]{1,0:T(8,128)(2,1)} %trained.1, s32[64,144]{1,0:T(8,128)} %exponents.1), custom_call_target="tpu_custom_call" | custom-call | flops 4000000 | bytes 3000000 | tf_op jit(solution)/shard_map/pallas_call | solution.py:83
  1.7 5.5 %collective-permute-start = (bf16[144,4096]{1,0:T(8,128)(2,1)S(1)}, bf16[144,4096]{1,0:T(8,128)(2,1)S(1)}, u32[]{:S(2)}, u32[]{:S(2)}) collective-permute-start(bf16[144,4096]{1,0:T(8,128)(2,1)S(1)} %get-tuple-element.14), channel_id=1, source_target_pairs={{0,48},{48,0},{96,144},{144,96},{192,240},{240,192},{288,336},{336... | collective-permute-start | bytes 3538952 | tf_op jit(solution)/shard_map/ppermute | solution.py:197
  7.1 0.1 convert_element_type.9
  7.2 0.0 copy-start.1
  7.2 33.4 %all-gather.1 = f16[4096,384]{1,0:T(8,128)(2,1)S(1)} all-gather(f16[512,384]{1,0:T(8,128)(2,1)S(1)} %convert_element_type.9), channel_id=1, replica_groups={{0,96,192,288,384,480,576,672},{48,144,240,336,432,528,624,720},{1,97,1..., dimensions={0}, use_global_device_ids=true | all-gather | bytes 3538944 | tf_op jit(solution)/shard_map/all_gather | solution.py:198
  40.7 0.0 copy-start
  40.7 0.0 collective-permute-done.got
  40.7 9.1 %collective-permute-start.1 = (bf16[144,4096]{1,0:T(8,128)(2,1)S(1)}, bf16[144,4096]{1,0:T(8,128)(2,1)S(1)}, u32[]{:S(2)}, u32[]{:S(2)}) collective-permute-start(bf16[144,4096]{1,0:T(8,128)(2,1)S(1)} %collective-permute-done.got), channel_id=1, source_target_pairs={{0,1},{1,0},{2,3},{3,2},{4,5},{5,4},{6,7},{7,6},{8,9},{9,8},{10,11... | collective-permute-start | bytes 3538952 | tf_op jit(solution)/shard_map/ppermute | solution.py:200
  49.8 0.8 %multiply_convert_fusion.delta = bf16[4096,384]{1,0:T(8,128)(2,1)S(1)} fusion(f16[4096,384]{1,0:T(8,128)(2,1)S(1)} %all-gather.1), kind=kLoop, calls=%fused_computation | loop fusion | flops 4718592 | bytes 6291456 | tf_op jit(solution)/shard_map/convert_element_type | solution.py:201
  50.6 0.0 slice-start
  50.6 0.0 copy-done.1
  50.6 0.0 copy-done
  50.6 0.0 slice-start.1
  50.7 1.3 %shard_map.56 = (bf16[4096,384]{1,0:T(8,128)(2,1)S(1)}, bf16[144,384]{1,0:T(8,128)(2,1)S(1)}) custom-call(bf16[8,2,512,384]{3,2,1,0:T(8,128)(2,1)S(1)} %bitcast.1, bf16[4096,384]{1,0:T(8,128)(2,1)S(1)} %multiply_convert_fusion.delta, bf16[144,4096]{1,0:T(8,128)(2,1)S(1)} %collective-permute-done.got, bf16[8192]{0:T(1024)(128)(2,1)S(1)} %copy-done.1), custom_call_target="tpu_custom_call" | custom-call | flops 500000000 | bytes 8000000 | tf_op jit(solution)/shard_map/pallas_call | solution.py:149
  52.0 0.3 collective-permute-done.1.rest
  52.3 0.8 %shard_map.57.after = bf16[288,384]{1,0:T(8,128)(2,1)S(1)} custom-call(bf16[4096,384]{1,0:T(8,128)(2,1)S(1)} %get-tuple-element.17.weight, bf16[144,4096]{1,0:T(8,128)(2,1)S(1)} %collective-permute-done.1.rest, bf16[8192]{0:T(1024)(128)(2,1)S(1)} %copy-done.1, bf16[144,384]{1,0:T(8,128)(2,1)S(1)} %get-tuple-element.18.first), custom_call_target="tpu_custom_call" | custom-call | flops 500000000 | bytes 8000000 | tf_op jit(solution)/shard_map/pallas_call | solution.py:149
  53.1 4.8 %collective-permute-start.2 = (bf16[288,384]{1,0:T(8,128)(2,1)S(1)}, bf16[288,384]{1,0:T(8,128)(2,1)S(1)}, u32[]{:S(2)}, u32[]{:S(2)}) collective-permute-start(bf16[288,384]{1,0:T(8,128)(2,1)S(1)} %shard_map.57.after), channel_id=1, source_target_pairs={{0,48},{48,0},{96,144},{144,96},{192,240},{240,192},{288,336},{336... | collective-permute-start | bytes 663560 | tf_op jit(solution)/shard_map/ppermute | solution.py:215
  57.9 0.0 slice-done
  57.9 0.0 slice-done.1
  58.0 2.4 %shard_map.58 = (f32[288,384]{1,0:T(8,128)S(1)}, f32[288,128]{1,0:T(8,128)S(1)}) custom-call(bf16[288,8192]{1,0:T(8,128)(2,1)S(1)} %bitcast.3, bf16[4096,384]{1,0:T(8,128)(2,1)S(1)} %get-tuple-element.17.weight, bf16[8192]{0:T(1024)(128)(2,1)S(1)} %copy-done.1, bf16[288,384]{1,0:T(8,128)(2,1)S(1)} %shard_map.57.after), custom_call_target="tpu_custom_call" | custom-call | flops 1000000000 | bytes 8000000 | tf_op jit(solution)/shard_map/pallas_call | solution.py:149
  60.4 2.8 %collective-permute-done.2.far = bf16[288,384]{1,0:T(8,128)(2,1)S(1)} collective-permute-done((bf16[288,384]{1,0:T(8,128)(2,1)S(1)}, bf16[288,384]{1,0:T(8,128)(2,1)S(1)}, u32[]{:S(2)}, u32[]{:S(2)}) %collective-permute-start.2) | collective-permute-done | bytes 221216 | tf_op jit(solution)/shard_map/ppermute | solution.py:215
  63.1 0.9 %shard_map.59 = bf16[288,384]{1,0:T(8,128)(2,1)} custom-call(f32[288,384]{1,0:T(8,128)S(1)} %get-tuple-element.19.near, f32[288,128]{1,0:T(8,128)S(1)} %get-tuple-element.20.factor, bf16[288,384]{1,0:T(8,128)(2,1)S(1)} %collective-permute-done.2.far), custom_call_target="tpu_custom_call" | custom-call | flops 1000000 | bytes 1000000 | tf_op jit(solution)/shard_map/pallas_call | solution.py:175
  (1 shorter events, 0.0 us)
Async XLA Ops:
  1.7 39.0 %collective-permute-start = (bf16[144,4096]{1,0:T(8,128)(2,1)S(1)}, bf16[144,4096]{1,0:T(8,128)(2,1)S(1)}, u32[]{:S(2)}, u32[]{:S(2)}) collective-permute-start(bf16[144,4096]{1,0:T(8,128)(2,1)S(1)} %get-tuple-element.14), channel_id=1, source_target_pairs={{0,48},{48,0},{96,144},{144,96},{192,240},{240,192},{288,336},{336... | collective-permute-start | bytes 3538952 | tf_op jit(solution)/shard_map/ppermute | solution.py:197
  7.2 43.4 %copy-start.1 = (bf16[8192]{0:T(1024)(128)(2,1)S(1)}, bf16[8192]{0:T(1024)(128)(2,1)}, u32[]{:S(2)}) copy-start(bf16[8192]{0:T(1024)(128)(2,1)} %gain.5) | copy-start | bytes 49156
  40.7 10.0 %copy-start = (bf16[8192,384]{1,0:T(8,128)(2,1)S(1)}, bf16[8192,384]{1,0:T(8,128)(2,1)}, u32[]{:S(2)}) copy-start(bf16[8192,384]{1,0:T(8,128)(2,1)} %base.1) | copy-start | bytes 18874372
  40.7 11.6 %collective-permute-start.1 = (bf16[144,4096]{1,0:T(8,128)(2,1)S(1)}, bf16[144,4096]{1,0:T(8,128)(2,1)S(1)}, u32[]{:S(2)}, u32[]{:S(2)}) collective-permute-start(bf16[144,4096]{1,0:T(8,128)(2,1)S(1)} %collective-permute-done.got), channel_id=1, source_target_pairs={{0,1},{1,0},{2,3},{3,2},{4,5},{5,4},{6,7},{7,6},{8,9},{9,8},{10,11... | collective-permute-start | bytes 3538952 | tf_op jit(solution)/shard_map/ppermute | solution.py:200
  50.6 7.3 %slice-start = ((s8[4718592]{0:T(1024)(128)(4,1)}), s8[4194304]{0:T(1024)(128)(4,1)S(1)}, s32[]{:S(2)}) async-start(s8[4718592]{0:T(1024)(128)(4,1)} %bitcast.2), calls=%async_computation | async-start | bytes 8388608
  50.6 7.3 %slice-start.1 = ((s8[4718592]{0:T(1024)(128)(4,1)}), s8[524288]{0:T(1024)(128)(4,1)S(1)}, s32[]{:S(2)}) async-start(s8[4718592]{0:T(1024)(128)(4,1)} %bitcast.2), calls=%async_computation.1 | async-start | bytes 1048576
  53.1 10.0 %collective-permute-start.2 = (bf16[288,384]{1,0:T(8,128)(2,1)S(1)}, bf16[288,384]{1,0:T(8,128)(2,1)S(1)}, u32[]{:S(2)}, u32[]{:S(2)}) collective-permute-start(bf16[288,384]{1,0:T(8,128)(2,1)S(1)} %shard_map.57.after), channel_id=1, source_target_pairs={{0,48},{48,0},{96,144},{144,96},{192,240},{240,192},{288,336},{336... | collective-permute-start | bytes 663560 | tf_op jit(solution)/shard_map/ppermute | solution.py:215
